TPU v7x, 512 devices: a whole 4x4x16 slice. The times are simulated.
512 devices in a mesh: grp: 16 (over y, x), tile: 32 (over z, core).
Axes of the slice: x: 4, y: 4, z: 16, core: 2. Of those that a mesh axis runs over, the one named last changes fastest.
Arguments:
- latent: bfloat16 [8, 64, 64, 512], P(None, 'grp', 'tile'), may hold values from -36 to 36
- coarse_filters: bfloat16 [3, 3, 3, 512, 512], P(None, None, None, None, 'grp'), may hold values from -0.0546875 to 0.0546875
- mid_filters: bfloat16 [3, 3, 3, 256, 256], P(None, None, None, None, 'tile'), may hold values from -0.078125 to 0.078125
- fine_filters: bfloat16 [3, 3, 3, 128, 128], replicated, may hold values from -0.109375 to 0.109375
- coarse_proj: bfloat16 [512, 256], replicated, may hold values from -0.25 to 0.25
- mid_proj: bfloat16 [256, 128], replicated, may hold values from -0.375 to 0.375
Outputs:
- frames_out: bfloat16 [8, 256, 256, 128], P(None, 'grp', 'tile')
All inputs are finite; a program needn't handle non-finite values.
Results may differ from a plain program's by a relative error of at most 0.018.
Values may be sent and summed in bfloat16 or wider, within the bound.
A program may use at most 128 MiB of HBM per device.

v0:
```python
import jax
import jax.numpy as jnp
from jax import lax
from jax.sharding import PartitionSpec as P


def with_halo(shard, sides, width):
    for axis, dim in sides:
        size, length = (lax.axis_size(axis), shard.shape[dim])
        up = [(i, (i + 1) % size) for i in range(size - 1)]
        down = [(j, i) for i, j in up]
        last = lax.slice_in_dim(shard, length - width, length, axis=dim)
        initial = lax.slice_in_dim(shard, 0, width, axis=dim)
        before = lax.ppermute(last, axis, up)
        after = lax.ppermute(initial, axis, down)
        shard = jnp.concatenate([before, shard, after], axis=dim)
    return shard


def activate(values):
    widened = values.astype(jnp.float32)
    scaled = widened * lax.rsqrt(jnp.mean(widened * widened, axis=-1, keepdims=True) + 1e-06)
    return jax.nn.silu(scaled).astype(jnp.bfloat16)


def double_size(values):
    return jnp.repeat(jnp.repeat(values, 2, axis=1), 2, axis=2)


def time_padded(values):
    return jnp.pad(values, ((2, 0), (0, 0), (0, 0), (0, 0)))


def stencil_columns(extended):
    padded = time_padded(extended)
    height = extended.shape[1] - 2
    breadth = extended.shape[2] - 2
    return jnp.concatenate(
        [
            padded[:, row_step : row_step + height, col_step : col_step + breadth, :]
            for row_step in range(3)
            for col_step in range(3)
        ],
        axis=-1,
    )


def apply_columns(columns, filters):
    frames = columns.shape[0] - 2
    folded = filters.reshape(3, 9 * filters.shape[3], filters.shape[4])
    total = jnp.dot(columns[0:frames], folded[0], preferred_element_type=jnp.float32)
    for frame_step in (1, 2):
        total = total + jnp.dot(
            columns[frame_step : frame_step + frames],
            folded[frame_step],
            preferred_element_type=jnp.float32,
        )
    return total


def coarse_conv(extended, filters):
    padded = time_padded(extended)
    frames = extended.shape[0]
    height = extended.shape[1] - 2
    breadth = extended.shape[2] - 2
    inputs = filters.shape[3]
    outputs = filters.shape[4]
    total = jnp.zeros((frames, height, breadth, outputs), jnp.float32)
    for frame_step in range(3):
        spread = jnp.transpose(filters[frame_step], (2, 0, 1, 3)).reshape(inputs, 9 * outputs)
        products = jnp.dot(
            padded[frame_step : frame_step + frames], spread, preferred_element_type=jnp.float32
        )
        for row_step in range(3):
            for col_step in range(3):
                lane = 3 * row_step + col_step
                total = (
                    total
                    + products[
                        :,
                        row_step : row_step + height,
                        col_step : col_step + breadth,
                        lane * outputs : (lane + 1) * outputs,
                    ]
                )
    return total


def middle_conv(extended, mid_filters):
    columns = stencil_columns(extended)
    return apply_columns(columns, lax.all_gather(mid_filters, "tile", axis=4, tiled=True))


def body(latent, coarse_filters, mid_filters, fine_filters, coarse_proj, mid_proj):
    first_act = activate(latent)
    whole = lax.all_gather(first_act, "grp", axis=1, tiled=True)
    widened = with_halo(whole, (("tile", 2),), 1)
    padded = jnp.pad(widened, ((0, 0), (1, 1), (0, 0), (0, 0)))
    filtered = coarse_conv(padded, coarse_filters).astype(jnp.bfloat16)
    returned = lax.all_to_all(filtered, "grp", split_axis=1, concat_axis=3, tiled=True)
    level_zero = (latent.astype(jnp.float32) + returned.astype(jnp.float32)).astype(jnp.bfloat16)
    reduced = jnp.dot(level_zero, coarse_proj, preferred_element_type=jnp.float32).astype(
        jnp.bfloat16
    )
    mid_act = double_size(activate(reduced))
    mid_ext = with_halo(mid_act, (("grp", 1), ("tile", 2)), 1)
    mid_terms = middle_conv(mid_ext, mid_filters)
    mid_out = (double_size(reduced).astype(jnp.float32) + mid_terms).astype(jnp.bfloat16)
    fine_low = jnp.dot(mid_out, mid_proj, preferred_element_type=jnp.float32).astype(jnp.bfloat16)
    fine_in = double_size(fine_low)
    fine_act = double_size(activate(fine_low))
    fine_ext = with_halo(fine_act, (("grp", 1), ("tile", 2)), 1)
    fine_terms = apply_columns(stencil_columns(fine_ext), fine_filters)
    return (fine_in.astype(jnp.float32) + fine_terms).astype(jnp.bfloat16)


def solution(mesh):
    in_specs = (
        P(None, "grp", "tile", None),
        P(None, None, None, None, "grp"),
        P(None, None, None, None, "tile"),
        P(),
        P(),
        P(),
    )
    out_specs = P(None, "grp", "tile", None)
    return jax.shard_map(body, mesh=mesh, in_specs=in_specs, out_specs=out_specs, check_vma=False)
```

profile of v0, /device:TPU:1, one launch (start us, length us, event | category | flops | bytes accessed | tf_op | source)
XLA Modules:
  0.0 199.0 jit_solution(11646952750403236550)
XLA Ops:
  6.5 1.0 fusion.34
  7.6 1.6 fusion.33
  9.3 0.7 all-gather.5.cloned.1.call-update
  10.0 62.3 %all-gather.3.cloned.1.call-done = bf16[8,64,2,512]{3,0,2,1:T(8,128)(2,1)} async-done(((bf16[8,4,2,512]{3,0,2,1:T(8,128)(2,1)}), bf16[8,64,2,512]{3,0,2,1:T(8,128)(2,1)}) %all-gather.3.cloned.1.call-update) | async-done | bytes 1048592 | tf_op jit(solution)/shard_map/all_gather | solution.py:96
  72.3 1.8 copy.25
  74.2 5.2 %collective-permute-start = (bf16[8,64,1,512]{3,1,2,0:T(8,128)(2,1)S(1)}, bf16[8,64,1,512]{3,1,2,0:T(8,128)(2,1)S(1)}, u32[]{:S(2)}, u32[]{:S(2)}) collective-permute-start(bf16[8,64,1,512]{3,1,2,0:T(8,128)(2,1)S(1)} %get-tuple-element.8), channel_id=1, source_target_pairs={{0,1},{1,2},{2,3},{3,4},{4,5},{5,6},{6,7},{7,8},{8,9},{9,10},{10,1... | collective-permute-start | bytes 1572872 | tf_op jit(solution)/shard_map/ppermute | solution.py:14
  79.4 1.9 collective-permute-start.1
  81.4 4.1 %collective-permute-done = bf16[8,64,1,512]{3,1,2,0:T(8,128)(2,1)S(1)} collective-permute-done((bf16[8,64,1,512]{3,1,2,0:T(8,128)(2,1)S(1)}, bf16[8,64,1,512]{3,1,2,0:T(8,128)(2,1)S(1)}, u32[]{:S(2)}, u32[]{:S(2)}) %collective-permute-start) | collective-permute-done | bytes 524320 | tf_op jit(solution)/shard_map/ppermute | solution.py:14
  85.5 4.4 %collective-permute-done.1 = bf16[8,64,1,512]{3,1,2,0:T(8,128)(2,1)S(1)} collective-permute-done((bf16[8,64,1,512]{3,1,2,0:T(8,128)(2,1)S(1)}, bf16[8,64,1,512]{3,1,2,0:T(8,128)(2,1)S(1)}, u32[]{:S(2)}, u32[]{:S(2)}) %collective-permute-start.1) | collective-permute-done | bytes 524320 | tf_op jit(solution)/shard_map/ppermute | solution.py:15
  89.9 1.0 fusion.5
  90.9 1.4 fusion.47
  92.4 1.4 fusion.50
  93.8 1.4 fusion.51
  95.2 2.5 %fusion.24 = bf16[8,64,2,32]{3,1,2,0:T(8,128)(2,1)S(1)} fusion(f32[8,66,4,288]{3,1,2,0:T(8,128)S(1)} %fusion.47, f32[8,66,4,288]{3,1,2,0:T(8,128)S(1)} %fusion.51, f32[8,66,4,288]{3,1,2,0:T(8,128)S(1)} %fusion.50), kind=kLoop, calls=%fused_computation.35 | loop fusion | flops 884736 | bytes 3604480 | tf_op jit(solution)/shard_map/convert_element_type | solution.py:99
  97.8 0.3 copy.67
  98.0 0.3 reshape.91
  98.3 10.9 %all_to_all.4 = bf16[16,2,1024]{2,1,0:T(2,128)(2,1)S(1)} all-to-all(bf16[16,2,1024]{2,1,0:T(2,128)(2,1)S(1)} %reshape.91), channel_id=1, replica_groups=mesh['grp'=16,'tile'=32] {'grp'}, dimensions={0} | all-to-all | bytes 131072 | tf_op jit(solution)/shard_map/all_to_all | solution.py:100
  109.2 0.2 reshape.92
  109.4 0.2 copy.66
  109.5 0.2 reshape.78
  109.8 0.3 multiply_reduce_fusion.1
  110.4 2.2 %collective-permute-start.2 = (bf16[8,1,4,256]{3,2,1,0:T(4,128)(2,1)S(1)}, bf16[8,1,4,256]{3,2,1,0:T(4,128)(2,1)S(1)}, u32[]{:S(2)}, u32[]{:S(2)}) collective-permute-start(bf16[8,1,4,256]{3,2,1,0:T(4,128)(2,1)S(1)} %get-tuple-element.23), channel_id=1, source_target_pairs={{0,32},{32,64},{64,96},{96,128},{128,160},{160,192},{192,224},{224... | collective-permute-start | bytes 49160 | tf_op jit(solution)/shard_map/ppermute | solution.py:14
  112.6 1.3 collective-permute-start.3
  114.0 3.1 %collective-permute-done.3 = bf16[8,1,4,256]{3,2,1,0:T(4,128)(2,1)S(1)} collective-permute-done((bf16[8,1,4,256]{3,2,1,0:T(4,128)(2,1)S(1)}, bf16[8,1,4,256]{3,2,1,0:T(4,128)(2,1)S(1)}, u32[]{:S(2)}, u32[]{:S(2)}) %collective-permute-start.3) | collective-permute-done | bytes 16416 | tf_op jit(solution)/shard_map/ppermute | solution.py:15
  117.3 4.7 %collective-permute-start.4 = (bf16[8,10,1,256]{3,2,1,0:T(2,128)(2,1)S(1)}, bf16[8,10,1,256]{3,2,1,0:T(2,128)(2,1)S(1)}, u32[]{:S(2)}, u32[]{:S(2)}) collective-permute-start(bf16[8,10,1,256]{3,2,1,0:T(2,128)(2,1)S(1)} %get-tuple-element.20), channel_id=1, source_target_pairs={{0,1},{1,2},{2,3},{3,4},{4,5},{5,6},{6,7},{7,8},{8,9},{9,10},{10,1... | collective-permute-start | bytes 122888 | tf_op jit(solution)/shard_map/ppermute | solution.py:14
  121.9 2.1 %collective-permute-start.5 = (bf16[8,10,1,256]{3,2,1,0:T(2,128)(2,1)S(1)}, bf16[8,10,1,256]{3,2,1,0:T(2,128)(2,1)S(1)}, u32[]{:S(2)}, u32[]{:S(2)}) collective-permute-start(bf16[8,10,1,256]{3,2,1,0:T(2,128)(2,1)S(1)} %get-tuple-element.21), channel_id=1, source_target_pairs={{1,0},{2,1},{3,2},{4,3},{5,4},{6,5},{7,6},{8,7},{9,8},{10,9},{11,1... | collective-permute-start | bytes 122888 | tf_op jit(solution)/shard_map/ppermute | solution.py:15
  124.2 0.2 convert_element_type.86
  124.5 3.2 %collective-permute-done.5 = bf16[8,10,1,256]{3,2,1,0:T(2,128)(2,1)S(1)} collective-permute-done((bf16[8,10,1,256]{3,2,1,0:T(2,128)(2,1)S(1)}, bf16[8,10,1,256]{3,2,1,0:T(2,128)(2,1)S(1)}, u32[]{:S(2)}, u32[]{:S(2)}) %collective-permute-start.5) | collective-permute-done | bytes 40992 | tf_op jit(solution)/shard_map/ppermute | solution.py:15
  127.7 0.3 fusion.26
  128.0 0.7 slice_dynamic-update-slice_fusion.17
  128.7 0.8 slice_dynamic-update-slice_fusion.16
  129.5 0.8 slice_dynamic-update-slice_fusion.15
  130.4 0.8 slice_dynamic-update-slice_fusion.14
  131.1 0.8 slice_dynamic-update-slice_fusion.13
  131.9 0.8 slice_dynamic-update-slice_fusion.12
  132.7 0.8 slice_dynamic-update-slice_fusion.11
  133.5 0.8 slice_dynamic-update-slice_fusion.10
  134.3 0.8 slice_dynamic-update-slice_fusion.9
  135.1 18.5 %all-gather.5.cloned.1.call-done = bf16[3,3,3,256,256]{3,4,2,1,0:T(8,128)(2,1)} async-done(((bf16[3,3,3,256,8]{3,4,2,1,0:T(8,128)(2,1)}), bf16[3,3,3,256,256]{3,4,2,1,0:T(8,128)(2,1)}) %all-gather.5.cloned.1.call-update) | async-done | bytes 3538960 | tf_op jit(solution)/shard_map/all_gather | solution.py:91
  153.6 3.3 %fusion.40 = (bf16[1,3,3,256,256]{3,4,2,1,0:T(8,128)(2,1)S(1)}, bf16[1,3,3,256,256]{3,4,2,1,0:T(8,128)(2,1)S(1)}, bf16[1,3,3,256,256]{3,4,2,1,0:T(8,128)(2,1)}) fusion(bf16[3,3,3,256,256]{3,4,2,1,0:T(8,128)(2,1)} %all-gather.5.cloned.1.call-done), kind=kLoop, calls=%fused_computation.110 | loop fusion | bytes 7077888 | tf_op jit(solution)/shard_map/slice | solution.py:55
  156.9 2.4 %copy.49 = bf16[1,3,3,256,256]{4,3,2,1,0:T(8,128)(2,1)} copy(bf16[1,3,3,256,256]{3,4,2,1,0:T(8,128)(2,1)} %get-tuple-element.7) | data formatting | bytes 2359296
  159.3 1.6 copy.50
  160.9 0.7 copy.51
  161.6 2.4 %fusion.48 = f32[8,8,4,256]{3,2,1,0:T(4,128)S(1)} fusion(bf16[10,8,4,2304]{3,2,1,0:T(4,128)(2,1)} %slice_dynamic-update-slice_fusion.9, bf16[2304,256,1,1]{1,0,3,2:T(8,128)(2,1)} %bitcast.115), kind=kOutput, calls=%fused_computation.119 | convolution fusion | flops 301989888 | bytes 2916352 | tf_op jit(solution)/shard_map/dot_general | solution.py:51
  164.0 2.0 convolution_add_fusion.3
  166.0 2.1 %fusion.14 = bf16[8,8,4,256]{3,2,1,0:T(4,128)(2,1)S(1)} fusion(f32[8,8,4,256]{3,2,1,0:T(4,128)S(1)} %convert_element_type.86, f32[8,8,4,256]{3,2,1,0:T(4,128)S(1)} %convolution_add_fusion.3, bf16[10,8,4,2304]{3,2,1,0:T(4,128)(2,1)} %slice_dynamic-update-slice_fusion.9, bf16[2304,256,1,1]{1,0,3,2:T(8,128)(2,1)S(1)} %bitcast.114), kind=kOutput, calls=%fused_computation.21 | convolution fusion | flops 302186496 | bytes 3309568 | tf_op jit(solution)/shard_map/dot_general | solution.py:53
  168.1 0.3 multiply_reduce_fusion
  168.6 0.2 broadcast_in_dim.34
  168.8 3.0 %collective-permute-start.6 = (bf16[8,1,8,128]{3,2,1,0:T(8,128)(2,1)S(1)}, bf16[8,1,8,128]{3,2,1,0:T(8,128)(2,1)S(1)}, u32[]{:S(2)}, u32[]{:S(2)}) collective-permute-start(bf16[8,1,8,128]{3,2,1,0:T(8,128)(2,1)S(1)} %get-tuple-element.18), channel_id=1, source_target_pairs={{0,32},{32,64},{64,96},{96,128},{128,160},{160,192},{192,224},{224... | collective-permute-start | bytes 49160 | tf_op jit(solution)/shard_map/ppermute | solution.py:14
  171.8 1.3 collective-permute-start.7
  173.1 3.2 %collective-permute-done.7 = bf16[8,1,8,128]{3,2,1,0:T(8,128)(2,1)S(1)} collective-permute-done((bf16[8,1,8,128]{3,2,1,0:T(8,128)(2,1)S(1)}, bf16[8,1,8,128]{3,2,1,0:T(8,128)(2,1)S(1)}, u32[]{:S(2)}, u32[]{:S(2)}) %collective-permute-start.7) | collective-permute-done | bytes 16416 | tf_op jit(solution)/shard_map/ppermute | solution.py:15
  176.4 5.1 %collective-permute-start.8 = (bf16[8,18,1,128]{3,2,1,0:T(2,128)(2,1)S(1)}, bf16[8,18,1,128]{3,2,1,0:T(2,128)(2,1)S(1)}, u32[]{:S(2)}, u32[]{:S(2)}) collective-permute-start(bf16[8,18,1,128]{3,2,1,0:T(2,128)(2,1)S(1)} %get-tuple-element.16), channel_id=1, source_target_pairs={{0,1},{1,2},{2,3},{3,4},{4,5},{5,6},{6,7},{7,8},{8,9},{9,10},{10,1... | collective-permute-start | bytes 110600 | tf_op jit(solution)/shard_map/ppermute | solution.py:14
  181.5 1.9 collective-permute-start.9
  183.6 3.6 %collective-permute-done.9 = bf16[8,18,1,128]{3,2,1,0:T(2,128)(2,1)S(1)} collective-permute-done((bf16[8,18,1,128]{3,2,1,0:T(2,128)(2,1)S(1)}, bf16[8,18,1,128]{3,2,1,0:T(2,128)(2,1)S(1)}, u32[]{:S(2)}, u32[]{:S(2)}) %collective-permute-start.9) | collective-permute-done | bytes 36896 | tf_op jit(solution)/shard_map/ppermute | solution.py:15
  187.2 0.4 fusion.21
  187.6 0.2 slice_dynamic-update-slice_fusion.7
  187.8 0.2 slice_dynamic-update-slice_fusion.6
  188.1 0.2 slice_dynamic-update-slice_fusion.4
  188.2 0.2 slice_dynamic-update-slice_fusion.3
  188.5 0.1 slice_dynamic-update-slice_fusion.1
  188.8 0.8 fusion.49
  189.6 0.8 convolution_add_fusion.1
  190.5 0.2 broadcast_in_dim.32
  190.7 1.5 fusion.12
  (49 shorter events, 1.9 us)
Async XLA Ops:
  6.5 103.2 %copy-start = (bf16[512,256]{1,0:T(8,128)(2,1)S(1)}, bf16[512,256]{1,0:T(8,128)(2,1)}, u32[]{:S(2)}) copy-start(bf16[512,256]{1,0:T(8,128)(2,1)} %param.10) | copy-start | bytes 786436
  6.5 74.8 %copy-start.2 = (bf16[3,3,3,512,32]{3,4,2,1,0:T(8,128)(2,1)S(1)}, bf16[3,3,3,512,32]{3,4,2,1,0:T(8,128)(2,1)}, u32[]{:S(2)}) copy-start(bf16[3,3,3,512,32]{3,4,2,1,0:T(8,128)(2,1)} %param.7) | copy-start | bytes 2654212
  6.5 65.8 %all-gather.3.cloned.1.call-start = ((), (), s32[]{:S(2)}) async-start(), calls=%async_computation.1 | async-start | bytes 1114112 | tf_op jit(solution)/shard_map/all_gather | solution.py:96
  9.2 144.4 %all-gather.5.cloned.1.call-start = ((), (), s32[]{:S(2)}) async-start(), calls=%async_computation.2 | async-start | bytes 3649536 | tf_op jit(solution)/shard_map/all_gather | solution.py:91
  74.2 11.3 %collective-permute-start = (bf16[8,64,1,512]{3,1,2,0:T(8,128)(2,1)S(1)}, bf16[8,64,1,512]{3,1,2,0:T(8,128)(2,1)S(1)}, u32[]{:S(2)}, u32[]{:S(2)}) collective-permute-start(bf16[8,64,1,512]{3,1,2,0:T(8,128)(2,1)S(1)} %get-tuple-element.8), channel_id=1, source_target_pairs={{0,1},{1,2},{2,3},{3,4},{4,5},{5,6},{6,7},{7,8},{8,9},{9,10},{10,1... | collective-permute-start | bytes 1572872 | tf_op jit(solution)/shard_map/ppermute | solution.py:14
  79.4 10.5 %collective-permute-start.1 = (bf16[8,64,1,512]{3,1,2,0:T(8,128)(2,1)S(1)}, bf16[8,64,1,512]{3,1,2,0:T(8,128)(2,1)S(1)}, u32[]{:S(2)}, u32[]{:S(2)}) collective-permute-start(bf16[8,64,1,512]{3,1,2,0:T(8,128)(2,1)S(1)} %get-tuple-element.9), channel_id=1, source_target_pairs={{1,0},{2,1},{3,2},{4,3},{5,4},{6,5},{7,6},{8,7},{9,8},{10,9},{11,1... | collective-permute-start | bytes 1572872 | tf_op jit(solution)/shard_map/ppermute | solution.py:15
  97.7 12.0 %copy-start.4 = (bf16[8,4,2,512]{3,2,1,0:T(2,128)(2,1)S(1)}, bf16[8,4,2,512]{3,2,1,0:T(2,128)(2,1)}, u32[]{:S(2)}) copy-start(bf16[8,4,2,512]{3,2,1,0:T(2,128)(2,1)} %param.6) | copy-start | bytes 196612
  110.4 3.5 %collective-permute-start.2 = (bf16[8,1,4,256]{3,2,1,0:T(4,128)(2,1)S(1)}, bf16[8,1,4,256]{3,2,1,0:T(4,128)(2,1)S(1)}, u32[]{:S(2)}, u32[]{:S(2)}) collective-permute-start(bf16[8,1,4,256]{3,2,1,0:T(4,128)(2,1)S(1)} %get-tuple-element.23), channel_id=1, source_target_pairs={{0,32},{32,64},{64,96},{96,128},{128,160},{160,192},{192,224},{224... | collective-permute-start | bytes 49160 | tf_op jit(solution)/shard_map/ppermute | solution.py:14
  112.6 4.5 %collective-permute-start.3 = (bf16[8,1,4,256]{3,2,1,0:T(4,128)(2,1)S(1)}, bf16[8,1,4,256]{3,2,1,0:T(4,128)(2,1)S(1)}, u32[]{:S(2)}, u32[]{:S(2)}) collective-permute-start(bf16[8,1,4,256]{3,2,1,0:T(4,128)(2,1)S(1)} %get-tuple-element.22), channel_id=1, source_target_pairs={{32,0},{64,32},{96,64},{128,96},{160,128},{192,160},{224,192},{256... | collective-permute-start | bytes 49160 | tf_op jit(solution)/shard_map/ppermute | solution.py:15
  117.3 7.2 %collective-permute-start.4 = (bf16[8,10,1,256]{3,2,1,0:T(2,128)(2,1)S(1)}, bf16[8,10,1,256]{3,2,1,0:T(2,128)(2,1)S(1)}, u32[]{:S(2)}, u32[]{:S(2)}) collective-permute-start(bf16[8,10,1,256]{3,2,1,0:T(2,128)(2,1)S(1)} %get-tuple-element.20), channel_id=1, source_target_pairs={{0,1},{1,2},{2,3},{3,4},{4,5},{5,6},{6,7},{7,8},{8,9},{9,10},{10,1... | collective-permute-start | bytes 122888 | tf_op jit(solution)/shard_map/ppermute | solution.py:14
  121.9 5.8 %collective-permute-start.5 = (bf16[8,10,1,256]{3,2,1,0:T(2,128)(2,1)S(1)}, bf16[8,10,1,256]{3,2,1,0:T(2,128)(2,1)S(1)}, u32[]{:S(2)}, u32[]{:S(2)}) collective-permute-start(bf16[8,10,1,256]{3,2,1,0:T(2,128)(2,1)S(1)} %get-tuple-element.21), channel_id=1, source_target_pairs={{1,0},{2,1},{3,2},{4,3},{5,4},{6,5},{7,6},{8,7},{9,8},{10,9},{11,1... | collective-permute-start | bytes 122888 | tf_op jit(solution)/shard_map/ppermute | solution.py:15
  161.6 2.4 %copy-start.1 = (bf16[1,3,3,256,256]{4,3,2,1,0:T(8,128)(2,1)S(1)}, bf16[1,3,3,256,256]{4,3,2,1,0:T(8,128)(2,1)}, u32[]{:S(2)}) copy-start(bf16[1,3,3,256,256]{4,3,2,1,0:T(8,128)(2,1)} %copy.50) | copy-start | bytes 3538948
  166.0 2.1 %copy-start.5 = (bf16[256,128]{1,0:T(8,128)(2,1)S(1)}, bf16[256,128]{1,0:T(8,128)(2,1)}, u32[]{:S(2)}) copy-start(bf16[256,128]{1,0:T(8,128)(2,1)} %param.11) | copy-start | bytes 196612
  166.0 17.4 %copy-start.3 = (bf16[3,3,3,128,128]{4,3,2,1,0:T(8,128)(2,1)S(1)}, bf16[3,3,3,128,128]{4,3,2,1,0:T(8,128)(2,1)}, u32[]{:S(2)}) copy-start(bf16[3,3,3,128,128]{4,3,2,1,0:T(8,128)(2,1)} %param.9) | copy-start | bytes 2654212
  168.8 4.3 %collective-permute-start.6 = (bf16[8,1,8,128]{3,2,1,0:T(8,128)(2,1)S(1)}, bf16[8,1,8,128]{3,2,1,0:T(8,128)(2,1)S(1)}, u32[]{:S(2)}, u32[]{:S(2)}) collective-permute-start(bf16[8,1,8,128]{3,2,1,0:T(8,128)(2,1)S(1)} %get-tuple-element.18), channel_id=1, source_target_pairs={{0,32},{32,64},{64,96},{96,128},{128,160},{160,192},{192,224},{224... | collective-permute-start | bytes 49160 | tf_op jit(solution)/shard_map/ppermute | solution.py:14
  171.8 4.5 %collective-permute-start.7 = (bf16[8,1,8,128]{3,2,1,0:T(8,128)(2,1)S(1)}, bf16[8,1,8,128]{3,2,1,0:T(8,128)(2,1)S(1)}, u32[]{:S(2)}, u32[]{:S(2)}) collective-permute-start(bf16[8,1,8,128]{3,2,1,0:T(8,128)(2,1)S(1)} %get-tuple-element.19), channel_id=1, source_target_pairs={{32,0},{64,32},{96,64},{128,96},{160,128},{192,160},{224,192},{256... | collective-permute-start | bytes 49160 | tf_op jit(solution)/shard_map/ppermute | solution.py:15
  176.4 7.2 %collective-permute-start.8 = (bf16[8,18,1,128]{3,2,1,0:T(2,128)(2,1)S(1)}, bf16[8,18,1,128]{3,2,1,0:T(2,128)(2,1)S(1)}, u32[]{:S(2)}, u32[]{:S(2)}) collective-permute-start(bf16[8,18,1,128]{3,2,1,0:T(2,128)(2,1)S(1)} %get-tuple-element.16), channel_id=1, source_target_pairs={{0,1},{1,2},{2,3},{3,4},{4,5},{5,6},{6,7},{7,8},{8,9},{9,10},{10,1... | collective-permute-start | bytes 110600 | tf_op jit(solution)/shard_map/ppermute | solution.py:14
  181.5 5.7 %collective-permute-start.9 = (bf16[8,18,1,128]{3,2,1,0:T(2,128)(2,1)S(1)}, bf16[8,18,1,128]{3,2,1,0:T(2,128)(2,1)S(1)}, u32[]{:S(2)}, u32[]{:S(2)}) collective-permute-start(bf16[8,18,1,128]{3,2,1,0:T(2,128)(2,1)S(1)} %get-tuple-element.17), channel_id=1, source_target_pairs={{1,0},{2,1},{3,2},{4,3},{5,4},{6,5},{7,6},{8,7},{9,8},{10,9},{11,1... | collective-permute-start | bytes 110600 | tf_op jit(solution)/shard_map/ppermute | solution.py:15
Sparse Core Ops, SparseCore 0:
  10.4 61.8 all-gather.2
  74.3 79.2 all-gather.4
where the time goes:
time: 201 us; the launch traced here: 199 us
  waiting for transfers between devices  103 us (51%)
  starting transfers between devices  28.6 us (14%)
  local copies, waits for them, and re-layouts  20.9 us (10%)
  matrix products  14.4 us (7%)
  between operations  13.9 us (7%)
  blocking collectives  10.9 us (5%)
  other arithmetic  7.18 us (4%)
    all_gather x1, waiting for transfers between devices, body(): whole = lax.all_gather(first_act, 'grp', axis=1, tiled=True)  62.3 us
    ppermute x5, starting transfers between devices, with_halo(): before = lax.ppermute(last, axis, up)  20.1 us
    all_gather x1, waiting for transfers between devices, middle_conv(): lax.all_gather(mid_filters, 'tile', axis=4, tiled=True)  18.5 us
    ppermute x5, waiting for transfers between devices, with_halo(): after = lax.ppermute(initial, axis, down)  17.5 us
    unnamed x35, local copies, waits for them, and re-layouts  12.7 us
    all_to_all x1, blocking collectives, body(): lax.all_to_all(filtered, 'grp', split_axis=1, concat_axis=3, tiled=True)  10.9 us
    ppermute x5, starting transfers between devices, with_halo(): after = lax.ppermute(initial, axis, down)  8.53 us
    dot_general x4, matrix products, apply_columns(): jnp.dot(columns[frame_step:frame_step + frames], folded[frame_step], pref...  6.33 us
  transfers between devices with their start and end apart: 12, of which 8 were waited for; matrix products, arithmetic and copies ran while one was open for 10% of the time, Pallas kernels for 0%

commit v1 on v0

v1 whole, which is shorter than its diff:
```python
import jax
import jax.numpy as jnp
from jax import lax
from jax.experimental import pallas as pl
from jax.experimental.pallas import tpu as pltpu
from jax.sharding import PartitionSpec as P

MESH = pl.DeviceIdType.MESH
F32 = jnp.float32
BF16 = jnp.bfloat16
NY = 4
NX = 4
NG = 16
NT_DIMS = (((1,), (1,)), ((), ()))
NN_DIMS = (((1,), (0,)), ((), ()))
SHIFTS = ((-1, 0, 0), (0, 0, 1))


def activate(values):
    scaled = values * lax.rsqrt(jnp.mean(values * values, axis=-1, keepdims=True) + 1e-06)
    return scaled / (1.0 + jnp.exp(-scaled))


def lane_group(rows):
    return lax.broadcasted_iota(jnp.int32, (rows, 128), 1) // 32


def pack_four(parts):
    group = lane_group(8)
    frame = lax.broadcasted_iota(jnp.int32, (8, 128), 0)
    one_back = (group == 1) & (frame >= 1)
    two_back = (group == 2) & (frame >= 2)
    total = None
    for k in range(4):
        mixed = jnp.where(
            group == 0, parts[k], jnp.where(group == 1, parts[(k + 1) % 4], parts[(k + 2) % 4])
        )
        moved = jnp.where(
            group == 0,
            mixed,
            jnp.where(
                one_back,
                pltpu.roll(mixed, 1, 0),
                jnp.where(two_back, pltpu.roll(mixed, 2, 0), 0.0),
            ),
        )
        turned = pltpu.roll(moved, 32 * k, 1) if k else moved
        total = turned if total is None else total + turned
    return total


def swap_groups(parts):
    rows = parts[0].shape[0]
    group = lane_group(rows)

    def pick(options):
        return jnp.where(
            group == 0,
            options[0],
            jnp.where(group == 1, options[1], jnp.where(group == 2, options[2], options[3])),
        )

    turned = []
    for k in range(4):
        mixed = pick([parts[(q + k) % 4] for q in range(4)])
        turned.append(pltpu.roll(mixed, 32 * k, 1) if k else mixed)
    return [pick([turned[(p - i) % 4] for p in range(4)]) for i in range(4)]


def frames_back(values, steps):
    frame = lax.broadcasted_iota(jnp.int32, values.shape, 1)
    return jnp.where(frame >= steps, pltpu.roll(values, steps, 1), 0.0)


def make_kernel(nz):
    nt = 2 * nz
    outs = 256 // nt
    half_ring = nz // 2

    def kernel(
        latent, cw_hbm, mw, fw_hbm, cproj, mproj, out,
        lat, gath, cw, prod, edge_out, edge_in, main, a2a_out, a2a_in,
        mine, theirs, wm, level, mact, mcol, mcor, mrow_in, mcol_in, mcor_in,
        mx3, mprod, fw, flow, fx, frow, fcol, fcor, frow_in, fcol_in, fcor_in, fprod, result,
        local_sem, send_sem, g1_sem, g2_sem, sib_sem, ring_sem, share_sem,
        edge_sem, a2a_sem, mh_sem, fh_sem,
    ):
        g = lax.axis_index("grp")
        t = lax.axis_index("tile")
        y, x = g // NX, g % NX
        z, core = t // 2, t % 2
        up_g, down_g = (g + NG - 1) % NG, (g + 1) % NG
        left_t, right_t = (t + nt - 1) % nt, (t + 1) % nt
        sib_t = z * 2 + 1 - core

        def gid(yy, xx):
            return ((yy + NY) % NY) * NX + (xx + NX) % NX

        def ring_t(dz):
            return ((z + dz + nz) % nz) * 2 + core

        sent = []

        def remote(src, dst, sem, dev):
            return pltpu.make_async_remote_copy(
                src_ref=src, dst_ref=dst, send_sem=send_sem.at[len(sent)], recv_sem=sem,
                device_id=dev, device_id_type=MESH,
            )

        def send(src, dst, sem, dev):
            copy = remote(src, dst, sem, dev)
            copy.start()
            sent.append(copy)

        def arrived(dst, sem):
            pltpu.make_async_remote_copy(
                src_ref=dst, dst_ref=dst, send_sem=send_sem.at[0], recv_sem=sem,
                device_id=(g, left_t), device_id_type=MESH,
            ).wait_recv()

        barrier = pltpu.get_barrier_semaphore()
        partners = [((g + d) % NG, t) for d in range(1, NG)]
        partners += [(g, left_t), (g, right_t), (g, ring_t(1)), (g, ring_t(-1))]
        partners += [(a, b) for a in (up_g, down_g) for b in (left_t, right_t)]
        for dev in partners:
            pl.semaphore_signal(barrier, inc=1, device_id=dev, device_id_type=MESH)

        locals_ = []
        for a in range(3):
            locals_.append(
                pltpu.make_async_copy(
                    cw_hbm.at[a], cw.at[:, pl.ds(32 * (2 - a), 32), :], local_sem.at[a]
                )
            )
            locals_.append(
                pltpu.make_async_copy(
                    fw_hbm.at[a], fw.at[:, pl.ds(128 * a, 128), :], local_sem.at[3 + a]
                )
            )
        for copy in locals_:
            copy.start()

        for f in range(8):
            cells = latent[f].astype(F32).reshape(8, 512)
            for big in range(4):
                lat[big, pl.ds(8 * f, 8), :] = cells[:, 128 * big : 128 * big + 128]

        def lat_cell(big, cell):
            return lat[big, pl.ds(cell, 8, stride=8), :]

        own_lat = jnp.concatenate(
            [
                jnp.concatenate([lat_cell(big, cell) for big in range(4)], axis=1)
                for cell in range(8)
            ],
            axis=0,
        )
        gath[g] = activate(own_lat).astype(BF16)
        own_mw = jnp.concatenate(
            [mw[...].astype(F32), jnp.zeros((1, outs, 256), F32)], axis=0
        )
        mine[...] = own_mw.reshape(28 * outs, 256).astype(BF16)
        cw[:, pl.ds(96, 32), :] = jnp.zeros((9, 32, 512), BF16)
        prod[:, 0] = jnp.zeros((9, 16, 128), F32)
        prod[:, 65] = jnp.zeros((9, 16, 128), F32)

        pl.semaphore_wait(barrier, len(partners))

        def near(h, axis, d):
            along_x = (axis == 1) == (h == 0)
            return (gid(y, x + d), t) if along_x else (gid(y + d, x), t)

        def shard(h, d1, d2):
            return gid(y + d2, x + d1) if h == 0 else gid(y + d1, x + d2)

        def part(h, d1, d2, first, count):
            return gath.at[shard(h, d1, d2), pl.ds(32 * h + first, count), :]

        steps = (0, -1, 1, 2)

        def second(h, k):
            src = part(h, steps[k], 0, 0, 32)
            send(src, src, g2_sem.at[h, k, 0], near(h, 2, 1))
            send(src, src, g2_sem.at[h, k, 1], near(h, 2, -1))

        def pass_on(h, k):
            arrived(part(h, steps[k], -1, 0, 32), g2_sem.at[h, k, 0])
            src = part(h, steps[k], -1, 0, 16)
            send(src, src, g2_sem.at[h, k, 2], near(h, 2, 1))
            arrived(part(h, steps[k], 1, 0, 32), g2_sem.at[h, k, 1])
            src = part(h, steps[k], 1, 16, 16)
            send(src, src, g2_sem.at[h, k, 3], near(h, 2, -1))

        for h in range(2):
            src = part(h, 0, 0, 0, 32)
            send(src, src, g1_sem.at[h, 0], near(h, 1, 1))
            send(src, src, g1_sem.at[h, 1], near(h, 1, -1))
        send(mine, theirs, sib_sem.at[0], (g, sib_t))
        for h in range(2):
            second(h, 0)

        arrived(theirs, sib_sem.at[0])
        own_f = mine[...].astype(F32).reshape(28, outs, 256)
        other_f = theirs[...].astype(F32).reshape(28, outs, 256)
        even = (jnp.zeros((1, 1, 256), jnp.int32) + core) == 0
        joined = jnp.concatenate(
            [jnp.where(even, own_f, other_f), jnp.where(even, other_f, own_f)], axis=1
        )
        rows_z = pl.multiple_of(2 * outs * z, 16)
        for a in range(3):
            for qh in range(2):
                wm[:, pl.ds(rows_z, 2 * outs), pl.ds(384 * qh + 128 * a, 128)] = joined[
                    9 * a : 9 * a + 9, :, 128 * qh : 128 * qh + 128
                ].astype(BF16)

        def block(dz):
            row = pl.multiple_of(2 * outs * ((z + dz + nz) % nz), 16)
            lane = pl.multiple_of(384 * core, 128)
            return wm.at[:, pl.ds(row, 2 * outs), pl.ds(lane, 384)]

        def sib_block(dz):
            row = pl.multiple_of(2 * outs * ((z + dz + nz) % nz), 16)
            lane = pl.multiple_of(384 * (1 - core), 128)
            return wm.at[:, pl.ds(row, 2 * outs), pl.ds(lane, 384)]

        sign = 1 - 2 * core

        def ring_send(k):
            if k < half_ring:
                send(block(1 - k), block(1 - k), ring_sem.at[0, k], (g, ring_t(1)))
                send(block(k - 1), block(k - 1), ring_sem.at[1, k], (g, ring_t(-1)))
            elif k == half_ring:
                src = block(-sign * (k - 1))
                send(src, src, ring_sem.at[0, k], (g, ring_t(sign)))

        def share(dz, slot):
            send(block(dz), block(dz), share_sem.at[slot], (g, sib_t))

        def ring_step(k):
            if k < half_ring:
                arrived(block(-k), ring_sem.at[0, k])
                arrived(block(k), ring_sem.at[1, k])
                ring_send(k + 1)
                share(-k, 2 * k)
                share(k, 2 * k + 1)
            elif k == half_ring:
                arrived(block(k), ring_sem.at[0, k])
                share(k, 2 * k)

        ring_send(1)

        for h in range(2):
            arrived(part(h, -1, 0, 0, 32), g1_sem.at[h, 0])
            src = part(h, -1, 0, 0, 16)
            send(src, src, g1_sem.at[h, 2], near(h, 1, 1))
            arrived(part(h, 1, 0, 0, 32), g1_sem.at[h, 1])
            src = part(h, 1, 0, 16, 16)
            send(src, src, g1_sem.at[h, 3], near(h, 1, -1))
        for h in range(2):
            second(h, 1)
            second(h, 2)
        for h in range(2):
            pass_on(h, 0)
        for h in range(2):
            arrived(part(h, 2, 0, 0, 16), g1_sem.at[h, 2])
            arrived(part(h, 2, 0, 16, 16), g1_sem.at[h, 3])
            second(h, 3)
        ring_step(1)
        for k in (1, 2):
            for h in range(2):
                pass_on(h, k)
        for h in range(2):
            pass_on(h, 3)
        ring_step(2)
        for h in range(2):
            for k in range(4):
                arrived(part(h, steps[k], 2, 0, 16), g2_sem.at[h, k, 2])
                arrived(part(h, steps[k], 2, 16, 16), g2_sem.at[h, k, 3])
        for copy in locals_:
            copy.wait()

        def coarse_rows(q, _):
            acts = gath[pl.ds(4 * q, 4)].reshape(256, 512)
            for b in range(3):
                found = lax.dot_general(
                    acts, cw[pl.ds(3 * b, 3)].reshape(384, 512), NT_DIMS,
                    preferred_element_type=F32,
                )
                for c in range(3):
                    prod[3 * b + c, pl.ds(16 * q + 1, 16)] = found[
                        :, 128 * c : 128 * c + 128
                    ].reshape(16, 16, 128)
            return 0

        lax.fori_loop(0, 2, coarse_rows, 0)
        ring_step(3)
        lax.fori_loop(2, 4, coarse_rows, 0)

        def taps(row, c, j):
            return sum(prod[3 * b + c, row + b, pl.ds(8 * j, 8), :] for b in range(3))

        def edges(rr, _):
            for e, (c, j) in enumerate(((2, 0), (0, 1))):
                both = [
                    pack_four([taps(8 * rr + 4 * s + i, c, j) for i in range(4)]) for s in range(2)
                ]
                edge_out[e, rr] = jnp.concatenate(both, axis=0).astype(BF16)
            return 0

        lax.fori_loop(0, 8, edges, 0)
        send(edge_out.at[0], edge_in.at[1], edge_sem.at[1], (g, left_t))
        send(edge_out.at[1], edge_in.at[0], edge_sem.at[0], (g, right_t))

        def mains(r, _):
            for j in range(2):
                main[r, pl.ds(8 * j, 8), :] = pack_four(
                    [
                        taps(4 * r + i, 1, j) + taps(4 * r + i, 2 if j == 0 else 0, 1 - j)
                        for i in range(4)
                    ]
                )
            return 0

        lax.fori_loop(0, 16, mains, 0)
        ring_step(4)

        def inside(condition, like):
            return (jnp.zeros(like, jnp.int32) + condition.astype(jnp.int32)) > 0

        has_left, has_right = t > 0, t < nt - 1
        has_up, has_down = g > 0, g < NG - 1

        for j, has in ((0, has_left), (1, has_right)):
            arrived(edge_in.at[j], edge_sem.at[j])
            added = edge_in[j].astype(F32).reshape(16, 8, 128)
            added = jnp.where(inside(has, (16, 8, 128)), added, 0.0)
            main[:, pl.ds(8 * j, 8), :] = main[:, pl.ds(8 * j, 8), :] + added
        a2a_out[...] = main[...].astype(BF16)

        for d in range(1, NG):
            r = (g + d) % NG
            send(a2a_out.at[r], a2a_in.at[g], a2a_sem.at[d], (r, t))
        a2a_in[g] = a2a_out[g]
        ring_step(5)
        for d in range(1, NG):
            arrived(a2a_in.at[(g + NG - d) % NG], a2a_sem.at[d])

        for big in range(4):
            found = swap_groups([a2a_in[4 * big + p].astype(F32) for p in range(4)])
            for i in range(4):
                cells = jnp.concatenate(
                    [
                        lat_cell(big, 2 * i + j)
                        for j in range(2)
                    ],
                    axis=0,
                )
                level[pl.ds(16 * i, 16), pl.ds(128 * big, 128)] = (cells + found[i]).astype(BF16)
        reduced = jnp.dot(level[...], cproj[...], preferred_element_type=F32)
        reduced = reduced.astype(BF16).astype(F32)
        act = activate(reduced)
        mact[...] = act.astype(BF16)
        cells = act.reshape(8, 8, 256)
        for j in range(2):
            mcol[j] = jnp.concatenate(
                [act[16 * i + 8 * j : 16 * i + 8 * j + 8] for i in range(4)], axis=0
            ).astype(BF16)
            for i in range(2):
                corner = cells[6 * i + j]
                mcor[2 * i + j] = jnp.concatenate([corner, corner], axis=0).astype(BF16)

        def halo(row_first, row_last, col, cor, row_in, col_in, cor_in, sem):
            send(col.at[0], col_in.at[1], sem.at[3], (g, left_t))
            send(col.at[1], col_in.at[0], sem.at[2], (g, right_t))
            send(row_first, row_in.at[1], sem.at[1], (up_g, t))
            send(row_last, row_in.at[0], sem.at[0], (down_g, t))
            send(cor.at[0], cor_in.at[3], sem.at[7], (up_g, left_t))
            send(cor.at[1], cor_in.at[2], sem.at[6], (up_g, right_t))
            send(cor.at[2], cor_in.at[1], sem.at[5], (down_g, left_t))
            send(cor.at[3], cor_in.at[0], sem.at[4], (down_g, right_t))

        def halo_wait(row_in, col_in, cor_in, sem):
            for i in range(2):
                arrived(row_in.at[i], sem.at[i])
                arrived(col_in.at[i], sem.at[2 + i])
            for i in range(4):
                arrived(cor_in.at[i], sem.at[4 + i])

        halo(
            mact.at[pl.ds(0, 16)], mact.at[pl.ds(48, 16)], mcol, mcor,
            mrow_in, mcol_in, mcor_in, mh_sem,
        )
        for k in range(6, half_ring + 1):
            ring_step(k)
        halo_wait(mrow_in, mcol_in, mcor_in, mh_sem)

        def surround(center, row_in, col_in, cor_in, height, breadth):
            lanes = row_in.shape[-1]

            def keep(values, *conditions):
                for condition in conditions:
                    values = jnp.where(inside(condition, values.shape), values, 0.0)
                return values

            above = keep(row_in[0].astype(F32), has_up).reshape(breadth, 8, lanes)
            below = keep(row_in[1].astype(F32), has_down).reshape(breadth, 8, lanes)
            left = keep(col_in[0].astype(F32), has_left).reshape(height, 8, lanes)
            right = keep(col_in[1].astype(F32), has_right).reshape(height, 8, lanes)
            corner = [
                keep(cor_in[2 * i + j].astype(F32)[0:8], (has_up, has_down)[i], (has_left, has_right)[j])
                for i in range(2)
                for j in range(2)
            ]
            tiles = [corner[0]] + [above[j] for j in range(breadth)] + [corner[1]]
            for i in range(height):
                tiles += [left[i]] + [center(i, j) for j in range(breadth)] + [right[i]]
            tiles += [corner[2]] + [below[j] for j in range(breadth)] + [corner[3]]
            return jnp.concatenate([tile[None] for tile in tiles], axis=0)

        around = surround(
            lambda i, j: cells[2 * i + j], mrow_in, mcol_in, mcor_in, 4, 2
        )
        for a in range(3):
            moved = frames_back(around, 2 - a) if a < 2 else around
            moved = moved.reshape(192, 256).astype(BF16)
            for qh in range(2):
                mx3[:, pl.ds(384 * qh + 128 * a, 128)] = moved[:, 128 * qh : 128 * qh + 128]

        for k in range(1, half_ring):
            arrived(sib_block(-k), share_sem.at[2 * k])
            arrived(sib_block(k), share_sem.at[2 * k + 1])
        arrived(sib_block(half_ring), share_sem.at[2 * half_ring])

        def mid_tap(bc, _):
            mprod[bc] = lax.dot_general(
                mx3[...], wm[bc], NT_DIMS, preferred_element_type=F32
            ).reshape(6, 4, 8, 256)
            return 0

        lax.fori_loop(0, 9, mid_tap, 0)

        def upsampled(products, height, breadth, pr, pc, residual):
            total = residual
            for b in range(3):
                low = 1 + SHIFTS[pr][b]
                for c in range(3):
                    side = 1 + SHIFTS[pc][c]
                    total = total + products[
                        3 * b + c, pl.ds(low, height), pl.ds(side, breadth)
                    ]
            return total

        residual = reduced.reshape(4, 2, 8, 256)
        for pr in range(2):
            for pc in range(2):
                middle = upsampled(mprod, 4, 2, pr, pc, residual).astype(BF16).reshape(64, 256)
                low = jnp.dot(middle, mproj[...], preferred_element_type=F32)
                low = low.astype(BF16).astype(F32)
                lively = activate(low)
                for i in range(4):
                    for j in range(2):
                        at = 16 * i + 8 * j
                        flow[2 * i + pr, 2 * j + pc] = low[at : at + 8]
                        fx[2 * i + pr, 2 * j + pc] = lively[at : at + 8]

        frow[0] = fx[0].reshape(32, 128).astype(BF16)
        frow[1] = fx[7].reshape(32, 128).astype(BF16)
        fcol[0] = fx[:, 0].reshape(64, 128).astype(BF16)
        fcol[1] = fx[:, 3].reshape(64, 128).astype(BF16)
        for i in range(2):
            for j in range(2):
                corner = fx[7 * i, 3 * j]
                fcor[2 * i + j] = jnp.concatenate([corner, corner], axis=0).astype(BF16)
        halo(frow.at[0], frow.at[1], fcol, fcor, frow_in, fcol_in, fcor_in, fh_sem)
        halo_wait(frow_in, fcol_in, fcor_in, fh_sem)

        around = surround(lambda i, j: fx[i, j], frow_in, fcol_in, fcor_in, 8, 4)
        fine = jnp.concatenate(
            [
                (frames_back(around, 2 - a) if a < 2 else around).reshape(480, 128).astype(BF16)
                for a in range(3)
            ],
            axis=1,
        )
        for pair in range(5):
            names = [bc for bc in (2 * pair, 2 * pair + 1) if bc < 9]
            filters = jnp.concatenate([fw[bc] for bc in names], axis=1)
            found = lax.dot_general(fine, filters, NN_DIMS, preferred_element_type=F32)
            for n, bc in enumerate(names):
                fprod[bc] = found[:, 128 * n : 128 * n + 128].reshape(10, 6, 8, 128)

        for pr in range(2):
            for pc in range(2):
                for i in range(8):
                    for j in range(4):
                        total = flow[i, j]
                        for b in range(3):
                            for c in range(3):
                                total = total + fprod[
                                    3 * b + c, i + 1 + SHIFTS[pr][b], j + 1 + SHIFTS[pc][c]
                                ]
                        spot = 8 * (2 * i + pr) + 2 * j + pc
                        result[pl.ds(spot, 8, stride=128), :] = total
        out[...] = result[...].astype(BF16).reshape(8, 16, 8, 128)

        for copy in sent:
            copy.wait_send()

    return kernel


def count_sends(nz):
    ring = 2 * (nz // 2 - 1) + 1
    return 8 + 32 + 1 + 2 * ring + 2 + 15 + 16


def body(latent, coarse_filters, mid_filters, fine_filters, coarse_proj, mid_proj):
    nz = lax.axis_size("tile") // 2
    outs = mid_filters.shape[4]
    cw = jnp.transpose(coarse_filters, (0, 1, 2, 4, 3)).reshape(3, 9, 32, 512)
    mw = jnp.transpose(mid_filters, (0, 1, 2, 4, 3)).reshape(27, outs, 256)
    fw = fine_filters.reshape(3, 9, 128, 128)
    vmem = pl.BlockSpec(memory_space=pltpu.VMEM)
    anywhere = pl.BlockSpec(memory_space=pl.ANY)
    half = nz // 2
    dma = pltpu.SemaphoreType.DMA
    return pl.pallas_call(
        make_kernel(nz),
        out_shape=jax.ShapeDtypeStruct((8, 16, 8, 128), BF16),
        in_specs=[vmem, anywhere, vmem, anywhere, vmem, vmem],
        out_specs=vmem,
        scratch_shapes=[
            pltpu.VMEM((4, 64, 128), F32),
            pltpu.VMEM((16, 64, 512), BF16),
            pltpu.VMEM((9, 128, 512), BF16),
            pltpu.VMEM((9, 66, 16, 128), F32),
            pltpu.VMEM((2, 8, 16, 128), BF16),
            pltpu.VMEM((2, 8, 16, 128), BF16),
            pltpu.VMEM((16, 16, 128), F32),
            pltpu.VMEM((16, 16, 128), BF16),
            pltpu.VMEM((16, 16, 128), BF16),
            pltpu.VMEM((28 * outs, 256), BF16),
            pltpu.VMEM((28 * outs, 256), BF16),
            pltpu.VMEM((9, 256, 768), BF16),
            pltpu.VMEM((64, 512), BF16),
            pltpu.VMEM((64, 256), BF16),
            pltpu.VMEM((2, 32, 256), BF16),
            pltpu.VMEM((4, 16, 256), BF16),
            pltpu.VMEM((2, 16, 256), BF16),
            pltpu.VMEM((2, 32, 256), BF16),
            pltpu.VMEM((4, 16, 256), BF16),
            pltpu.VMEM((192, 768), BF16),
            pltpu.VMEM((9, 6, 4, 8, 256), F32),
            pltpu.VMEM((9, 384, 128), BF16),
            pltpu.VMEM((8, 4, 8, 128), F32),
            pltpu.VMEM((8, 4, 8, 128), F32),
            pltpu.VMEM((2, 32, 128), BF16),
            pltpu.VMEM((2, 64, 128), BF16),
            pltpu.VMEM((4, 16, 128), BF16),
            pltpu.VMEM((2, 32, 128), BF16),
            pltpu.VMEM((2, 64, 128), BF16),
            pltpu.VMEM((4, 16, 128), BF16),
            pltpu.VMEM((9, 10, 6, 8, 128), F32),
            pltpu.VMEM((1024, 128), F32),
            dma((6,)),
            dma((count_sends(nz),)),
            dma((2, 4)),
            dma((2, 4, 4)),
            dma((1,)),
            dma((2, half + 1)),
            dma((2 * half + 1,)),
            dma((2,)),
            dma((16,)),
            dma((8,)),
            dma((8,)),
        ],
        compiler_params=pltpu.CompilerParams(
            collective_id=0, has_side_effects=True, vmem_limit_bytes=50 * 1024 * 1024
        ),
    )(latent, cw, mw, fw, coarse_proj, mid_proj)


def solution(mesh):
    in_specs = (
        P(None, "grp", "tile", None),
        P(None, None, None, None, "grp"),
        P(None, None, None, None, "tile"),
        P(),
        P(),
        P(),
    )
    out_specs = P(None, "grp", "tile", None)
    return jax.shard_map(body, mesh=mesh, in_specs=in_specs, out_specs=out_specs, check_vma=False)
```

time: 201 us -> 73.4 us (0.37)
  waiting for transfers between devices: 103 us -> 0 us
  Pallas kernels: 0 us -> 66.5 us
  starting transfers between devices: 28.6 us -> 0 us
  matrix products: 14.4 us -> 0 us
  local copies, waits for them, and re-layouts: 20.9 us -> 6.56 us
  between operations: 13.9 us -> 0.02 us
  blocking collectives: 10.9 us -> 0 us
  other arithmetic: 7.18 us -> 0 us
    all_gather x2 -> x0, waiting for transfers between devices: 80.8 us -> none  [the longest x1 62.3 us: body(): whole = lax.all_gather(first_act, 'grp', axis=1, tiled=True)]
    pallas_call x0 -> x1, Pallas kernels: none -> 66.5 us  [body(): pl.pallas_call(make_kernel(nz), out_shape=jax.ShapeDtypeStruct((8, 16, 8,...]
    ppermute x10 -> x0, starting transfers between devices: 28.6 us -> none  [the longest x5 20.1 us: with_halo(): before = lax.ppermute(last, axis, up)]
    ppermute x10 -> x0, waiting for transfers between devices: 21.6 us -> none  [the longest x5 17.5 us: with_halo(): after = lax.ppermute(initial, axis, down)]
    dot_general x11 -> x0, matrix products: 14.4 us -> none  [the longest x4 6.33 us: apply_columns(): jnp.dot(columns[frame_step:frame_step + frames], folded[frame_step], pref...]
    all_to_all x1 -> x0, blocking collectives: 10.9 us -> none  [body(): lax.all_to_all(filtered, 'grp', split_axis=1, concat_axis=3, tiled=True)]
    unnamed x35 -> x13, local copies, waits for them, and re-layouts: 12.7 us -> 6.56 us
    convert_element_type x4 -> x0, other arithmetic: 4.31 us -> none  [the longest x1 2.5 us: body(): filtered = coarse_conv(padded, coarse_filters).astype(jnp.bfloat16)]
  transfers between devices with their start and end apart: 12 -> 0, of which waited for: 8 -> 0; matrix products, arithmetic and copies ran while one was open for 10% -> 0% of each run, Pallas kernels for 0% -> 0%
where the time goes in v1:
time: 73.4 us; the launch traced here: 73.1 us
  Pallas kernels  66.5 us (91%)
  local copies, waits for them, and re-layouts  6.56 us (9%)
    pallas_call x1, Pallas kernels, body(): pl.pallas_call(make_kernel(nz), out_shape=jax.ShapeDtypeStruct((8, 16, 8,...  66.5 us
    unnamed x13, local copies, waits for them, and re-layouts  6.56 us

profile of v1, /device:TPU:1, one launch (start us, length us, event | category | flops | bytes accessed | tf_op | source)
XLA Modules:
  0.0 73.1 jit_solution(14765226582805819986)
XLA Ops:
  0.0 0.0 copy-start
  0.0 1.2 %copy-done = bf16[3,3,3,512,32]{3,4,2,1,0:T(8,128)(2,1)S(1)} copy-done((bf16[3,3,3,512,32]{3,4,2,1,0:T(8,128)(2,1)S(1)}, bf16[3,3,3,512,32]{3,4,2,1,0:T(8,128)(2,1)}, u32[]{:S(2)}) %copy-start) | copy-done | bytes 884760
  1.2 0.0 copy-start.1
  1.2 1.2 %copy-done.1 = bf16[3,3,3,128,128]{4,3,2,1,0:T(8,128)(2,1)S(1)} copy-done((bf16[3,3,3,128,128]{4,3,2,1,0:T(8,128)(2,1)S(1)}, bf16[3,3,3,128,128]{4,3,2,1,0:T(8,128)(2,1)}, u32[]{:S(2)}) %copy-start.1) | copy-done | bytes 884760
  2.3 0.0 copy-start.2
  2.3 0.9 %copy-done.2 = bf16[512,256]{1,0:T(8,128)(2,1)S(1)} copy-done((bf16[512,256]{1,0:T(8,128)(2,1)S(1)}, bf16[512,256]{1,0:T(8,128)(2,1)}, u32[]{:S(2)}) %copy-start.2) | copy-done | bytes 262168
  3.3 0.0 copy-start.3
  3.3 0.9 %copy-done.3 = bf16[3,3,3,256,8]{3,4,2,1,0:T(8,128)(2,1)S(1)} copy-done((bf16[3,3,3,256,8]{3,4,2,1,0:T(8,128)(2,1)S(1)}, bf16[3,3,3,256,8]{3,4,2,1,0:T(8,128)(2,1)}, u32[]{:S(2)}) %copy-start.3) | copy-done | bytes 110616
  4.2 0.0 copy-start.4
  4.2 0.8 %copy-done.4 = bf16[8,4,2,512]{3,2,1,0:T(2,128)(2,1)S(1)} copy-done((bf16[8,4,2,512]{3,2,1,0:T(2,128)(2,1)S(1)}, bf16[8,4,2,512]{3,2,1,0:T(2,128)(2,1)}, u32[]{:S(2)}) %copy-start.4) | copy-done | bytes 65560
  5.0 0.0 copy-start.5
  5.0 0.8 %copy-done.5 = bf16[256,128]{1,0:T(8,128)(2,1)S(1)} copy-done((bf16[256,128]{1,0:T(8,128)(2,1)S(1)}, bf16[256,128]{1,0:T(8,128)(2,1)}, u32[]{:S(2)}) %copy-start.5) | copy-done | bytes 65560
  5.9 66.5 %shard_map.64 = bf16[8,16,8,128]{3,2,1,0:T(8,128)(2,1)S(1)} custom-call(bf16[8,4,2,512]{3,2,1,0:T(2,128)(2,1)S(1)} %copy-done.4, bf16[3,9,32,512]{3,2,1,0:T(8,128)(2,1)S(1)} %bitcast.7, bf16[27,8,256]{2,1,0:T(8,128)(2,1)S(1)} %bitcast.9, bf16[3,9,128,128]{3,2,1,0:T(8,128)(2,1)S(1)} %bitcast.8, bf16[512,256]{1,0:T(8,128)(2,1)S(1)} %copy-done.2, ...), custom_call_target="tpu_custom_call" | custom-call | tf_op jit(solution)/shard_map/pallas_call | solution.py:527
  72.4 0.7 copy.8
Async XLA Ops:
  0.0 1.2 %copy-start = (bf16[3,3,3,512,32]{3,4,2,1,0:T(8,128)(2,1)S(1)}, bf16[3,3,3,512,32]{3,4,2,1,0:T(8,128)(2,1)}, u32[]{:S(2)}) copy-start(bf16[3,3,3,512,32]{3,4,2,1,0:T(8,128)(2,1)} %param.7) | copy-start | bytes 2654212
  1.2 1.2 %copy-start.1 = (bf16[3,3,3,128,128]{4,3,2,1,0:T(8,128)(2,1)S(1)}, bf16[3,3,3,128,128]{4,3,2,1,0:T(8,128)(2,1)}, u32[]{:S(2)}) copy-start(bf16[3,3,3,128,128]{4,3,2,1,0:T(8,128)(2,1)} %param.9) | copy-start | bytes 2654212
  2.3 0.9 %copy-start.2 = (bf16[512,256]{1,0:T(8,128)(2,1)S(1)}, bf16[512,256]{1,0:T(8,128)(2,1)}, u32[]{:S(2)}) copy-start(bf16[512,256]{1,0:T(8,128)(2,1)} %cproj.1) | copy-start | bytes 786436
  3.3 0.9 %copy-start.3 = (bf16[3,3,3,256,8]{3,4,2,1,0:T(8,128)(2,1)S(1)}, bf16[3,3,3,256,8]{3,4,2,1,0:T(8,128)(2,1)}, u32[]{:S(2)}) copy-start(bf16[3,3,3,256,8]{3,4,2,1,0:T(8,128)(2,1)} %param.8) | copy-start | bytes 331780
  4.2 0.8 %copy-start.4 = (bf16[8,4,2,512]{3,2,1,0:T(2,128)(2,1)S(1)}, bf16[8,4,2,512]{3,2,1,0:T(2,128)(2,1)}, u32[]{:S(2)}) copy-start(bf16[8,4,2,512]{3,2,1,0:T(2,128)(2,1)} %latent.1) | copy-start | bytes 196612
  5.0 0.8 %copy-start.5 = (bf16[256,128]{1,0:T(8,128)(2,1)S(1)}, bf16[256,128]{1,0:T(8,128)(2,1)}, u32[]{:S(2)}) copy-start(bf16[256,128]{1,0:T(8,128)(2,1)} %mproj.1) | copy-start | bytes 196612

commit v2 on v1

--- a/solution.py
+++ b/solution.py
@@ -78,12 +78,12 @@
     half_ring = nz // 2
 
     def kernel(
-        latent, cw_hbm, mw, fw_hbm, cproj, mproj, out,
-        lat, gath, cw, prod, edge_out, edge_in, main, a2a_out, a2a_in,
-        mine, theirs, wm, level, mact, mcol, mcor, mrow_in, mcol_in, mcor_in,
-        mx3, mprod, fw, flow, fx, frow, fcol, fcor, frow_in, fcol_in, fcor_in, fprod, result,
+        latent_hbm, cw_hbm, mw_hbm, fw_hbm, cproj_hbm, mproj_hbm, out,
+        latent, mw, cproj, mproj, lat, gath, cw, prod, edge_out, edge_in, main, a2a_out, a2a_in,
+        mine, theirs, wm, level, mrow, mcol, mcor, mrow_in, mcol_in, mcor_in,
+        mx3, mprod, middle, fw, flow, fx, fprod, result,
         local_sem, send_sem, g1_sem, g2_sem, sib_sem, ring_sem, share_sem,
-        edge_sem, a2a_sem, mh_sem, fh_sem,
+        edge_sem, a2a_sem, mh_sem,
     ):
         g = lax.axis_index("grp")
         t = lax.axis_index("tile")
@@ -125,7 +125,14 @@
         for dev in partners:
             pl.semaphore_signal(barrier, inc=1, device_id=dev, device_id_type=MESH)
 
-        locals_ = []
+        early = [
+            pltpu.make_async_copy(latent_hbm, latent, local_sem.at[6]),
+            pltpu.make_async_copy(mw_hbm, mw, local_sem.at[7]),
+        ]
+        locals_ = [
+            pltpu.make_async_copy(cproj_hbm, cproj, local_sem.at[8]),
+            pltpu.make_async_copy(mproj_hbm, mproj, local_sem.at[9]),
+        ]
         for a in range(3):
             locals_.append(
                 pltpu.make_async_copy(
@@ -137,8 +144,10 @@
                     fw_hbm.at[a], fw.at[:, pl.ds(128 * a, 128), :], local_sem.at[3 + a]
                 )
             )
-        for copy in locals_:
+        for copy in early + locals_:
             copy.start()
+        for copy in early:
+            copy.wait()
 
         for f in range(8):
             cells = latent[f].astype(F32).reshape(8, 512)
@@ -177,25 +186,21 @@
             return gath.at[shard(h, d1, d2), pl.ds(32 * h + first, count), :]
 
         steps = (0, -1, 1, 2)
+        ways = (1, -1, 2)
+
+        def first(h):
+            src = part(h, 0, 0, 0, 32)
+            for n, way in enumerate(ways):
+                send(src, src, g1_sem.at[h, n], near(h, 1, way))
 
         def second(h, k):
             src = part(h, steps[k], 0, 0, 32)
-            send(src, src, g2_sem.at[h, k, 0], near(h, 2, 1))
-            send(src, src, g2_sem.at[h, k, 1], near(h, 2, -1))
-
-        def pass_on(h, k):
-            arrived(part(h, steps[k], -1, 0, 32), g2_sem.at[h, k, 0])
-            src = part(h, steps[k], -1, 0, 16)
-            send(src, src, g2_sem.at[h, k, 2], near(h, 2, 1))
-            arrived(part(h, steps[k], 1, 0, 32), g2_sem.at[h, k, 1])
-            src = part(h, steps[k], 1, 16, 16)
-            send(src, src, g2_sem.at[h, k, 3], near(h, 2, -1))
-
+            for n, way in enumerate(ways):
+                send(src, src, g2_sem.at[h, k, n], near(h, 2, way))
+
+        send(mine, theirs, sib_sem.at[0], (g, sib_t))
         for h in range(2):
-            src = part(h, 0, 0, 0, 32)
-            send(src, src, g1_sem.at[h, 0], near(h, 1, 1))
-            send(src, src, g1_sem.at[h, 1], near(h, 1, -1))
-        send(mine, theirs, sib_sem.at[0], (g, sib_t))
+            first(h)
         for h in range(2):
             second(h, 0)
 
@@ -213,88 +218,78 @@
                     9 * a : 9 * a + 9, :, 128 * qh : 128 * qh + 128
                 ].astype(BF16)
 
-        def block(dz):
+        cuts = ((0, 5), (5, 4))
+
+        def block(dz, core_at, cut=(0, 9)):
             row = pl.multiple_of(2 * outs * ((z + dz + nz) % nz), 16)
-            lane = pl.multiple_of(384 * core, 128)
-            return wm.at[:, pl.ds(row, 2 * outs), pl.ds(lane, 384)]
-
-        def sib_block(dz):
-            row = pl.multiple_of(2 * outs * ((z + dz + nz) % nz), 16)
-            lane = pl.multiple_of(384 * (1 - core), 128)
-            return wm.at[:, pl.ds(row, 2 * outs), pl.ds(lane, 384)]
+            lane = pl.multiple_of(384 * core_at, 128)
+            return wm.at[pl.ds(*cut), pl.ds(row, 2 * outs), pl.ds(lane, 384)]
 
         sign = 1 - 2 * core
 
-        def ring_send(k):
+        def ring_send(k, n):
             if k < half_ring:
-                send(block(1 - k), block(1 - k), ring_sem.at[0, k], (g, ring_t(1)))
-                send(block(k - 1), block(k - 1), ring_sem.at[1, k], (g, ring_t(-1)))
+                src = block(1 - k, core, cuts[n])
+                send(src, src, ring_sem.at[0, k, n], (g, ring_t(1)))
+                src = block(k - 1, core, cuts[n])
+                send(src, src, ring_sem.at[1, k, n], (g, ring_t(-1)))
             elif k == half_ring:
-                src = block(-sign * (k - 1))
-                send(src, src, ring_sem.at[0, k], (g, ring_t(sign)))
+                src = block(-sign * (k - 1), core, cuts[n])
+                send(src, src, ring_sem.at[0, k, n], (g, ring_t(sign)))
 
         def share(dz, slot):
-            send(block(dz), block(dz), share_sem.at[slot], (g, sib_t))
-
-        def ring_step(k):
+            src = block(dz, core)
+            send(src, src, share_sem.at[slot], (g, sib_t))
+
+        def ring_event(k, n):
+            arrived(block(-k, core, cuts[n]), ring_sem.at[0, k, n])
             if k < half_ring:
-                arrived(block(-k), ring_sem.at[0, k])
-                arrived(block(k), ring_sem.at[1, k])
-                ring_send(k + 1)
+                arrived(block(k, core, cuts[n]), ring_sem.at[1, k, n])
+            ring_send(k + 1, n)
+            if n == 1:
                 share(-k, 2 * k)
-                share(k, 2 * k + 1)
-            elif k == half_ring:
-                arrived(block(k), ring_sem.at[0, k])
-                share(k, 2 * k)
-
-        ring_send(1)
-
-        for h in range(2):
-            arrived(part(h, -1, 0, 0, 32), g1_sem.at[h, 0])
-            src = part(h, -1, 0, 0, 16)
-            send(src, src, g1_sem.at[h, 2], near(h, 1, 1))
-            arrived(part(h, 1, 0, 0, 32), g1_sem.at[h, 1])
-            src = part(h, 1, 0, 16, 16)
-            send(src, src, g1_sem.at[h, 3], near(h, 1, -1))
-        for h in range(2):
-            second(h, 1)
-            second(h, 2)
-        for h in range(2):
-            pass_on(h, 0)
-        for h in range(2):
-            arrived(part(h, 2, 0, 0, 16), g1_sem.at[h, 2])
-            arrived(part(h, 2, 0, 16, 16), g1_sem.at[h, 3])
-            second(h, 3)
-        ring_step(1)
-        for k in (1, 2):
-            for h in range(2):
-                pass_on(h, k)
-        for h in range(2):
-            pass_on(h, 3)
-        ring_step(2)
-        for h in range(2):
-            for k in range(4):
-                arrived(part(h, steps[k], 2, 0, 16), g2_sem.at[h, k, 2])
-                arrived(part(h, steps[k], 2, 16, 16), g2_sem.at[h, k, 3])
-        for copy in locals_:
-            copy.wait()
-
-        def coarse_rows(q, _):
-            acts = gath[pl.ds(4 * q, 4)].reshape(256, 512)
+                if k < half_ring:
+                    share(k, 2 * k + 1)
+
+        events = [(k, n) for k in range(1, half_ring + 1) for n in range(2)]
+
+        def poll(count):
+            for _ in range(min(count, len(events))):
+                ring_event(*events.pop(0))
+
+        for n in range(2):
+            ring_send(1, n)
+
+        def coarse_chunk(d2):
+            names = [(h, d1) for h in range(2) for d1 in steps]
+            acts = jnp.concatenate([part(h, d1, d2, 0, 32)[...] for h, d1 in names], axis=0)
             for b in range(3):
                 found = lax.dot_general(
                     acts, cw[pl.ds(3 * b, 3)].reshape(384, 512), NT_DIMS,
                     preferred_element_type=F32,
                 )
-                for c in range(3):
-                    prod[3 * b + c, pl.ds(16 * q + 1, 16)] = found[
-                        :, 128 * c : 128 * c + 128
-                    ].reshape(16, 16, 128)
-            return 0
-
-        lax.fori_loop(0, 2, coarse_rows, 0)
-        ring_step(3)
-        lax.fori_loop(2, 4, coarse_rows, 0)
+                for n, (h, d1) in enumerate(names):
+                    row = 4 * shard(h, d1, d2) + 2 * h + 1
+                    for c in range(3):
+                        prod[3 * b + c, pl.ds(row, 2)] = found[
+                            32 * n : 32 * n + 32, 128 * c : 128 * c + 128
+                        ].reshape(2, 16, 128)
+
+        for k in (1, 2, 3):
+            for h in range(2):
+                arrived(part(h, steps[k], 0, 0, 32), g1_sem.at[h, k - 1])
+                second(h, k)
+        for copy in locals_:
+            copy.wait()
+        coarse_chunk(0)
+        poll(2)
+        for n, way in enumerate(ways):
+            for k in range(4):
+                for h in range(2):
+                    arrived(part(h, steps[k], -way if n < 2 else 2, 0, 32), g2_sem.at[h, k, n])
+            coarse_chunk(-way if n < 2 else 2)
+            poll(1)
+        poll(1)
 
         def taps(row, c, j):
             return sum(prod[3 * b + c, row + b, pl.ds(8 * j, 8), :] for b in range(3))
@@ -308,6 +303,7 @@
             return 0
 
         lax.fori_loop(0, 8, edges, 0)
+        poll(1)
         send(edge_out.at[0], edge_in.at[1], edge_sem.at[1], (g, left_t))
         send(edge_out.at[1], edge_in.at[0], edge_sem.at[0], (g, right_t))
 
@@ -322,7 +318,7 @@
             return 0
 
         lax.fori_loop(0, 16, mains, 0)
-        ring_step(4)
+        poll(1)
 
         def inside(condition, like):
             return (jnp.zeros(like, jnp.int32) + condition.astype(jnp.int32)) > 0
@@ -341,7 +337,7 @@
             r = (g + d) % NG
             send(a2a_out.at[r], a2a_in.at[g], a2a_sem.at[d], (r, t))
         a2a_in[g] = a2a_out[g]
-        ring_step(5)
+        poll(3)
         for d in range(1, NG):
             arrived(a2a_in.at[(g + NG - d) % NG], a2a_sem.at[d])
 
@@ -358,12 +354,12 @@
                 level[pl.ds(16 * i, 16), pl.ds(128 * big, 128)] = (cells + found[i]).astype(BF16)
         reduced = jnp.dot(level[...], cproj[...], preferred_element_type=F32)
         reduced = reduced.astype(BF16).astype(F32)
-        act = activate(reduced)
-        mact[...] = act.astype(BF16)
-        cells = act.reshape(8, 8, 256)
+        mrow[0] = reduced[0:16].astype(BF16)
+        mrow[1] = reduced[48:64].astype(BF16)
+        cells = reduced.reshape(8, 8, 256)
         for j in range(2):
             mcol[j] = jnp.concatenate(
-                [act[16 * i + 8 * j : 16 * i + 8 * j + 8] for i in range(4)], axis=0
+                [reduced[16 * i + 8 * j : 16 * i + 8 * j + 8] for i in range(4)], axis=0
             ).astype(BF16)
             for i in range(2):
                 corner = cells[6 * i + j]
@@ -386,12 +382,8 @@
             for i in range(4):
                 arrived(cor_in.at[i], sem.at[4 + i])
 
-        halo(
-            mact.at[pl.ds(0, 16)], mact.at[pl.ds(48, 16)], mcol, mcor,
-            mrow_in, mcol_in, mcor_in, mh_sem,
-        )
-        for k in range(6, half_ring + 1):
-            ring_step(k)
+        halo(mrow.at[0], mrow.at[1], mcol, mcor, mrow_in, mcol_in, mcor_in, mh_sem)
+        poll(2)
         halo_wait(mrow_in, mcol_in, mcor_in, mh_sem)
 
         def surround(center, row_in, col_in, cor_in, height, breadth):
@@ -417,19 +409,19 @@
             tiles += [corner[2]] + [below[j] for j in range(breadth)] + [corner[3]]
             return jnp.concatenate([tile[None] for tile in tiles], axis=0)
 
-        around = surround(
-            lambda i, j: cells[2 * i + j], mrow_in, mcol_in, mcor_in, 4, 2
-        )
+        low = surround(lambda i, j: cells[2 * i + j], mrow_in, mcol_in, mcor_in, 4, 2)
+        around = activate(low)
         for a in range(3):
             moved = frames_back(around, 2 - a) if a < 2 else around
             moved = moved.reshape(192, 256).astype(BF16)
             for qh in range(2):
                 mx3[:, pl.ds(384 * qh + 128 * a, 128)] = moved[:, 128 * qh : 128 * qh + 128]
+        poll(len(events))
 
         for k in range(1, half_ring):
-            arrived(sib_block(-k), share_sem.at[2 * k])
-            arrived(sib_block(k), share_sem.at[2 * k + 1])
-        arrived(sib_block(half_ring), share_sem.at[2 * half_ring])
+            arrived(block(-k, 1 - core), share_sem.at[2 * k])
+            arrived(block(k, 1 - core), share_sem.at[2 * k + 1])
+        arrived(block(half_ring, 1 - core), share_sem.at[2 * half_ring])
 
         def mid_tap(bc, _):
             mprod[bc] = lax.dot_general(
@@ -439,42 +431,37 @@
 
         lax.fori_loop(0, 9, mid_tap, 0)
 
-        def upsampled(products, height, breadth, pr, pc, residual):
-            total = residual
-            for b in range(3):
-                low = 1 + SHIFTS[pr][b]
-                for c in range(3):
-                    side = 1 + SHIFTS[pc][c]
-                    total = total + products[
-                        3 * b + c, pl.ds(low, height), pl.ds(side, breadth)
-                    ]
-            return total
-
-        residual = reduced.reshape(4, 2, 8, 256)
+        low = low.reshape(6, 4, 8, 256)
         for pr in range(2):
             for pc in range(2):
-                middle = upsampled(mprod, 4, 2, pr, pc, residual).astype(BF16).reshape(64, 256)
-                low = jnp.dot(middle, mproj[...], preferred_element_type=F32)
-                low = low.astype(BF16).astype(F32)
-                lively = activate(low)
-                for i in range(4):
-                    for j in range(2):
-                        at = 16 * i + 8 * j
-                        flow[2 * i + pr, 2 * j + pc] = low[at : at + 8]
-                        fx[2 * i + pr, 2 * j + pc] = lively[at : at + 8]
-
-        frow[0] = fx[0].reshape(32, 128).astype(BF16)
-        frow[1] = fx[7].reshape(32, 128).astype(BF16)
-        fcol[0] = fx[:, 0].reshape(64, 128).astype(BF16)
-        fcol[1] = fx[:, 3].reshape(64, 128).astype(BF16)
-        for i in range(2):
-            for j in range(2):
-                corner = fx[7 * i, 3 * j]
-                fcor[2 * i + j] = jnp.concatenate([corner, corner], axis=0).astype(BF16)
-        halo(frow.at[0], frow.at[1], fcol, fcor, frow_in, fcol_in, fcor_in, fh_sem)
-        halo_wait(frow_in, fcol_in, fcor_in, fh_sem)
-
-        around = surround(lambda i, j: fx[i, j], frow_in, fcol_in, fcor_in, 8, 4)
+                total = low[1 - pr : 6 - pr, 1 - pc : 4 - pc]
+                for b in range(3):
+                    row = SHIFTS[pr][b] + 1 - pr
+                    for c in range(3):
+                        col = SHIFTS[pc][c] + 1 - pc
+                        total = total + mprod[3 * b + c, pl.ds(row, 5), pl.ds(col, 3)]
+                middle[pl.ds(120 * (2 * pr + pc), 120), :] = total.reshape(120, 256)
+        fine_low = jnp.dot(middle[...].astype(BF16), mproj[...], preferred_element_type=F32)
+        fine_low = fine_low.astype(BF16).astype(F32)
+        lively = activate(fine_low)
+        for pr in range(2):
+            for pc in range(2):
+                for i in range(5):
+                    for j in range(3):
+                        row, col = 2 * i + 1 - pr, 2 * j + 1 - pc
+                        at = 120 * (2 * pr + pc) + 8 * (3 * i + j)
+                        tile = lively[at : at + 8]
+                        for edge, has in (
+                            (row == 0, has_up), (row == 9, has_down),
+                            (col == 0, has_left), (col == 5, has_right),
+                        ):
+                            if edge:
+                                tile = jnp.where(inside(has, (8, 128)), tile, 0.0)
+                        fx[row, col] = tile
+                        if 1 <= row <= 8 and 1 <= col <= 4:
+                            flow[row - 1, col - 1] = fine_low[at : at + 8]
+
+        around = fx[...].reshape(60, 8, 128)
         fine = jnp.concatenate(
             [
                 (frames_back(around, 2 - a) if a < 2 else around).reshape(480, 128).astype(BF16)
@@ -511,7 +498,7 @@
 
 def count_sends(nz):
     ring = 2 * (nz // 2 - 1) + 1
-    return 8 + 32 + 1 + 2 * ring + 2 + 15 + 16
+    return 6 + 24 + 1 + 3 * ring + 2 + 15 + 8
 
 
 def body(latent, coarse_filters, mid_filters, fine_filters, coarse_proj, mid_proj):
@@ -521,15 +508,18 @@
     mw = jnp.transpose(mid_filters, (0, 1, 2, 4, 3)).reshape(27, outs, 256)
     fw = fine_filters.reshape(3, 9, 128, 128)
     vmem = pl.BlockSpec(memory_space=pltpu.VMEM)
-    anywhere = pl.BlockSpec(memory_space=pl.ANY)
     half = nz // 2
     dma = pltpu.SemaphoreType.DMA
     return pl.pallas_call(
         make_kernel(nz),
         out_shape=jax.ShapeDtypeStruct((8, 16, 8, 128), BF16),
-        in_specs=[vmem, anywhere, vmem, anywhere, vmem, vmem],
+        in_specs=[pl.BlockSpec(memory_space=pl.ANY)] * 6,
         out_specs=vmem,
         scratch_shapes=[
+            pltpu.VMEM((8, 4, 2, 512), BF16),
+            pltpu.VMEM((27, outs, 256), BF16),
+            pltpu.VMEM((512, 256), BF16),
+            pltpu.VMEM((256, 128), BF16),
             pltpu.VMEM((4, 64, 128), F32),
             pltpu.VMEM((16, 64, 512), BF16),
             pltpu.VMEM((9, 128, 512), BF16),
@@ -543,7 +533,7 @@
             pltpu.VMEM((28 * outs, 256), BF16),
             pltpu.VMEM((9, 256, 768), BF16),
             pltpu.VMEM((64, 512), BF16),
-            pltpu.VMEM((64, 256), BF16),
+            pltpu.VMEM((2, 16, 256), BF16),
             pltpu.VMEM((2, 32, 256), BF16),
             pltpu.VMEM((4, 16, 256), BF16),
             pltpu.VMEM((2, 16, 256), BF16),
@@ -551,31 +541,25 @@
             pltpu.VMEM((4, 16, 256), BF16),
             pltpu.VMEM((192, 768), BF16),
             pltpu.VMEM((9, 6, 4, 8, 256), F32),
+            pltpu.VMEM((480, 256), F32),
             pltpu.VMEM((9, 384, 128), BF16),
             pltpu.VMEM((8, 4, 8, 128), F32),
-            pltpu.VMEM((8, 4, 8, 128), F32),
-            pltpu.VMEM((2, 32, 128), BF16),
-            pltpu.VMEM((2, 64, 128), BF16),
-            pltpu.VMEM((4, 16, 128), BF16),
-            pltpu.VMEM((2, 32, 128), BF16),
-            pltpu.VMEM((2, 64, 128), BF16),
-            pltpu.VMEM((4, 16, 128), BF16),
+            pltpu.VMEM((10, 6, 8, 128), F32),
             pltpu.VMEM((9, 10, 6, 8, 128), F32),
             pltpu.VMEM((1024, 128), F32),
-            dma((6,)),
+            dma((10,)),
             dma((count_sends(nz),)),
-            dma((2, 4)),
-            dma((2, 4, 4)),
+            dma((2, 3)),
+            dma((2, 4, 3)),
             dma((1,)),
-            dma((2, half + 1)),
+            dma((2, half + 1, 2)),
             dma((2 * half + 1,)),
             dma((2,)),
             dma((16,)),
             dma((8,)),
-            dma((8,)),
         ],
         compiler_params=pltpu.CompilerParams(
-            collective_id=0, has_side_effects=True, vmem_limit_bytes=50 * 1024 * 1024
+            collective_id=0, has_side_effects=True, vmem_limit_bytes=60 * 1024 * 1024
         ),
     )(latent, cw, mw, fw, coarse_proj, mid_proj)
 

time: 73.4 us -> 61.3 us (0.84)
  Pallas kernels: 66.5 us -> 59.4 us
  local copies, waits for them, and re-layouts: 6.56 us -> 1.67 us
    pallas_call x1, Pallas kernels: 66.5 us -> 59.4 us  [body(): pl.pallas_call(make_kernel(nz), out_shape=jax.ShapeDtypeStruct((8, 16, 8,...]
    unnamed x13 -> x1, local copies, waits for them, and re-layouts: 6.56 us -> 1.67 us
where the time goes in v2:
time: 61.3 us; the launch traced here: 61.1 us
  Pallas kernels  59.4 us (97%)
  local copies, waits for them, and re-layouts  1.67 us (3%)
    pallas_call x1, Pallas kernels, body(): pl.pallas_call(make_kernel(nz), out_shape=jax.ShapeDtypeStruct((8, 16, 8,...  59.4 us
    unnamed x1, local copies, waits for them, and re-layouts  1.67 us

profile of v2, /device:TPU:1, one launch (start us, length us, event | category | flops | bytes accessed | tf_op | source)
XLA Modules:
  0.0 61.1 jit_solution(12037173830371188747)
XLA Ops:
  0.0 59.4 %shard_map.64 = bf16[8,16,8,128]{3,2,1,0:T(8,128)(2,1)} custom-call(bf16[8,4,2,512]{3,2,1,0:T(2,128)(2,1)} %latent_hbm.1, bf16[3,9,32,512]{3,2,1,0:T(8,128)(2,1)} %bitcast.7, bf16[27,8,256]{2,1,0:T(8,128)(2,1)} %bitcast.9, bf16[3,9,128,128]{3,2,1,0:T(8,128)(2,1)} %bitcast.8, bf16[512,256]{1,0:T(8,128)(2,1)} %cproj_hbm.1, bf16[256,128]{1,0:T(8,128)(2,1)} %mproj_hbm.1), custom_call_target="tpu_custom_call" | custom-call | tf_op jit(solution)/shard_map/pallas_call | solution.py:513
  59.4 1.7 %copy.8 = bf16[8,16,8,128]{3,2,1,0:T(8,128)(2,1)} copy(bf16[8,16,8,128]{3,2,1,0:T(8,128)(2,1)} %shard_map.64) | data formatting | bytes 524288

commit v3 on v2

--- a/solution.py
+++ b/solution.py
@@ -13,6 +13,7 @@
 NG = 16
 NT_DIMS = (((1,), (1,)), ((), ()))
 NN_DIMS = (((1,), (0,)), ((), ()))
+POLLS = (3, 2, 3, 2, 2, 2, 4, 2, 4)
 SHIFTS = ((-1, 0, 0), (0, 0, 1))
 
 
@@ -201,9 +202,6 @@
         send(mine, theirs, sib_sem.at[0], (g, sib_t))
         for h in range(2):
             first(h)
-        for h in range(2):
-            second(h, 0)
-
         arrived(theirs, sib_sem.at[0])
         own_f = mine[...].astype(F32).reshape(28, outs, 256)
         other_f = theirs[...].astype(F32).reshape(28, outs, 256)
@@ -211,54 +209,48 @@
         joined = jnp.concatenate(
             [jnp.where(even, own_f, other_f), jnp.where(even, other_f, own_f)], axis=1
         )
-        rows_z = pl.multiple_of(2 * outs * z, 16)
         for a in range(3):
             for qh in range(2):
-                wm[:, pl.ds(rows_z, 2 * outs), pl.ds(384 * qh + 128 * a, 128)] = joined[
+                wm[z, pl.ds(9 * qh, 9), :, pl.ds(128 * a, 128)] = joined[
                     9 * a : 9 * a + 9, :, 128 * qh : 128 * qh + 128
                 ].astype(BF16)
 
-        cuts = ((0, 5), (5, 4))
-
-        def block(dz, core_at, cut=(0, 9)):
-            row = pl.multiple_of(2 * outs * ((z + dz + nz) % nz), 16)
-            lane = pl.multiple_of(384 * core_at, 128)
-            return wm.at[pl.ds(*cut), pl.ds(row, 2 * outs), pl.ds(lane, 384)]
-
         sign = 1 - 2 * core
 
+        def block(dz, first, count):
+            return wm.at[(z + dz + nz) % nz, pl.ds(first, count)]
+
+        def ring_part(k, n, dz):
+            if k < half_ring:
+                return block(dz, 6 * n, 6)
+            return block(dz, 9 * core + 3 * n, 3)
+
         def ring_send(k, n):
-            if k < half_ring:
-                src = block(1 - k, core, cuts[n])
-                send(src, src, ring_sem.at[0, k, n], (g, ring_t(1)))
-                src = block(k - 1, core, cuts[n])
-                send(src, src, ring_sem.at[1, k, n], (g, ring_t(-1)))
-            elif k == half_ring:
-                src = block(-sign * (k - 1), core, cuts[n])
-                send(src, src, ring_sem.at[0, k, n], (g, ring_t(sign)))
-
-        def share(dz, slot):
-            src = block(dz, core)
-            send(src, src, share_sem.at[slot], (g, sib_t))
+            if k <= half_ring:
+                src = ring_part(k, n, -sign * (k - 1))
+                send(src, src, ring_sem.at[k, n], (g, ring_t(sign)))
 
         def ring_event(k, n):
-            arrived(block(-k, core, cuts[n]), ring_sem.at[0, k, n])
-            if k < half_ring:
-                arrived(block(k, core, cuts[n]), ring_sem.at[1, k, n])
-            ring_send(k + 1, n)
-            if n == 1:
-                share(-k, 2 * k)
-                if k < half_ring:
-                    share(k, 2 * k + 1)
-
-        events = [(k, n) for k in range(1, half_ring + 1) for n in range(2)]
+            arrived(ring_part(k, n, -sign * k), ring_sem.at[k, n])
+            if k + 1 < half_ring:
+                ring_send(k + 1, n)
+            elif k + 1 == half_ring and n == 2:
+                for m in range(3):
+                    ring_send(k + 1, m)
+            if n == 2:
+                src = block(-sign * k, 0, 18) if k < half_ring else block(k, 9 * core, 9)
+                send(src, src, share_sem.at[k], (g, sib_t))
+
+        events = [(k, n) for k in range(1, half_ring + 1) for n in range(3)]
 
         def poll(count):
             for _ in range(min(count, len(events))):
                 ring_event(*events.pop(0))
 
-        for n in range(2):
+        for n in range(3):
             ring_send(1, n)
+        for h in range(2):
+            second(h, 0)
 
         def coarse_chunk(d2):
             names = [(h, d1) for h in range(2) for d1 in steps]
@@ -282,14 +274,13 @@
         for copy in locals_:
             copy.wait()
         coarse_chunk(0)
-        poll(2)
+        poll(POLLS[0])
         for n, way in enumerate(ways):
             for k in range(4):
                 for h in range(2):
                     arrived(part(h, steps[k], -way if n < 2 else 2, 0, 32), g2_sem.at[h, k, n])
             coarse_chunk(-way if n < 2 else 2)
-            poll(1)
-        poll(1)
+            poll(POLLS[1 + n])
 
         def taps(row, c, j):
             return sum(prod[3 * b + c, row + b, pl.ds(8 * j, 8), :] for b in range(3))
@@ -303,9 +294,9 @@
             return 0
 
         lax.fori_loop(0, 8, edges, 0)
-        poll(1)
         send(edge_out.at[0], edge_in.at[1], edge_sem.at[1], (g, left_t))
         send(edge_out.at[1], edge_in.at[0], edge_sem.at[0], (g, right_t))
+        poll(POLLS[4])
 
         def mains(r, _):
             for j in range(2):
@@ -318,7 +309,7 @@
             return 0
 
         lax.fori_loop(0, 16, mains, 0)
-        poll(1)
+        poll(POLLS[5])
 
         def inside(condition, like):
             return (jnp.zeros(like, jnp.int32) + condition.astype(jnp.int32)) > 0
@@ -337,9 +328,10 @@
             r = (g + d) % NG
             send(a2a_out.at[r], a2a_in.at[g], a2a_sem.at[d], (r, t))
         a2a_in[g] = a2a_out[g]
-        poll(3)
+        poll(POLLS[6])
         for d in range(1, NG):
             arrived(a2a_in.at[(g + NG - d) % NG], a2a_sem.at[d])
+        poll(POLLS[7])
 
         for big in range(4):
             found = swap_groups([a2a_in[4 * big + p].astype(F32) for p in range(4)])
@@ -383,7 +375,7 @@
                 arrived(cor_in.at[i], sem.at[4 + i])
 
         halo(mrow.at[0], mrow.at[1], mcol, mcor, mrow_in, mcol_in, mcor_in, mh_sem)
-        poll(2)
+        poll(POLLS[8])
         halo_wait(mrow_in, mcol_in, mcor_in, mh_sem)
 
         def surround(center, row_in, col_in, cor_in, height, breadth):
@@ -419,13 +411,15 @@
         poll(len(events))
 
         for k in range(1, half_ring):
-            arrived(block(-k, 1 - core), share_sem.at[2 * k])
-            arrived(block(k, 1 - core), share_sem.at[2 * k + 1])
-        arrived(block(half_ring, 1 - core), share_sem.at[2 * half_ring])
+            arrived(block(sign * k, 0, 18), share_sem.at[k])
+        arrived(block(half_ring, 9 * (1 - core), 9), share_sem.at[half_ring])
 
         def mid_tap(bc, _):
+            filters = jnp.concatenate(
+                [wm[:, bc + 9 * qh].reshape(256, 384) for qh in range(2)], axis=1
+            )
             mprod[bc] = lax.dot_general(
-                mx3[...], wm[bc], NT_DIMS, preferred_element_type=F32
+                mx3[...], filters, NT_DIMS, preferred_element_type=F32
             ).reshape(6, 4, 8, 256)
             return 0
 
@@ -497,8 +491,7 @@
 
 
 def count_sends(nz):
-    ring = 2 * (nz // 2 - 1) + 1
-    return 6 + 24 + 1 + 3 * ring + 2 + 15 + 8
+    return 6 + 24 + 1 + 4 * (nz // 2) + 2 + 15 + 8
 
 
 def body(latent, coarse_filters, mid_filters, fine_filters, coarse_proj, mid_proj):
@@ -531,7 +524,7 @@
             pltpu.VMEM((16, 16, 128), BF16),
             pltpu.VMEM((28 * outs, 256), BF16),
             pltpu.VMEM((28 * outs, 256), BF16),
-            pltpu.VMEM((9, 256, 768), BF16),
+            pltpu.VMEM((nz, 18, 2 * outs, 384), BF16),
             pltpu.VMEM((64, 512), BF16),
             pltpu.VMEM((2, 16, 256), BF16),
             pltpu.VMEM((2, 32, 256), BF16),
@@ -552,8 +545,8 @@
             dma((2, 3)),
             dma((2, 4, 3)),
             dma((1,)),
-            dma((2, half + 1, 2)),
-            dma((2 * half + 1,)),
+            dma((half + 1, 3)),
+            dma((half + 1,)),
             dma((2,)),
             dma((16,)),
             dma((8,)),

time: 61.3 us -> 59.2 us (0.966)
  Pallas kernels: 59.4 us -> 57.4 us
    pallas_call x1, Pallas kernels: 59.4 us -> 57.4 us  [body(): pl.pallas_call(make_kernel(nz), out_shape=jax.ShapeDtypeStruct((8, 16, 8,...]
where the time goes in v3:
time: 59.2 us; the launch traced here: 59.1 us
  Pallas kernels  57.4 us (97%)
  local copies, waits for them, and re-layouts  1.67 us (3%)
    pallas_call x1, Pallas kernels, body(): pl.pallas_call(make_kernel(nz), out_shape=jax.ShapeDtypeStruct((8, 16, 8,...  57.4 us
    unnamed x1, local copies, waits for them, and re-layouts  1.67 us

profile of v3, /device:TPU:1, one launch (start us, length us, event | category | flops | bytes accessed | tf_op | source)
XLA Modules:
  0.0 59.1 jit_solution(13006087720560494661)
XLA Ops:
  0.0 57.4 %shard_map.64 = bf16[8,16,8,128]{3,2,1,0:T(8,128)(2,1)} custom-call(bf16[8,4,2,512]{3,2,1,0:T(2,128)(2,1)} %latent_hbm.1, bf16[3,9,32,512]{3,2,1,0:T(8,128)(2,1)} %bitcast.7, bf16[27,8,256]{2,1,0:T(8,128)(2,1)} %bitcast.9, bf16[3,9,128,128]{3,2,1,0:T(8,128)(2,1)} %bitcast.8, bf16[512,256]{1,0:T(8,128)(2,1)} %cproj_hbm.1, bf16[256,128]{1,0:T(8,128)(2,1)} %mproj_hbm.1), custom_call_target="tpu_custom_call" | custom-call | tf_op jit(solution)/shard_map/pallas_call | solution.py:506
  57.4 1.7 %copy.8 = bf16[8,16,8,128]{3,2,1,0:T(8,128)(2,1)} copy(bf16[8,16,8,128]{3,2,1,0:T(8,128)(2,1)} %shard_map.64) | data formatting | bytes 524288

commit v4 on v3

--- a/solution.py
+++ b/solution.py
@@ -13,7 +13,7 @@
 NG = 16
 NT_DIMS = (((1,), (1,)), ((), ()))
 NN_DIMS = (((1,), (0,)), ((), ()))
-POLLS = (3, 2, 3, 2, 2, 2, 4, 2, 4)
+POLLS = (3, 3, 3, 2, 2, 2, 3, 2, 4)
 SHIFTS = ((-1, 0, 0), (0, 0, 1))
 
 
@@ -119,6 +119,13 @@
                 device_id=(g, left_t), device_id_type=MESH,
             ).wait_recv()
 
+        early = [
+            pltpu.make_async_copy(latent_hbm, latent, local_sem.at[6]),
+            pltpu.make_async_copy(mw_hbm, mw, local_sem.at[7]),
+        ]
+        for copy in early:
+            copy.start()
+
         barrier = pltpu.get_barrier_semaphore()
         partners = [((g + d) % NG, t) for d in range(1, NG)]
         partners += [(g, left_t), (g, right_t), (g, ring_t(1)), (g, ring_t(-1))]
@@ -126,10 +133,6 @@
         for dev in partners:
             pl.semaphore_signal(barrier, inc=1, device_id=dev, device_id_type=MESH)
 
-        early = [
-            pltpu.make_async_copy(latent_hbm, latent, local_sem.at[6]),
-            pltpu.make_async_copy(mw_hbm, mw, local_sem.at[7]),
-        ]
         locals_ = [
             pltpu.make_async_copy(cproj_hbm, cproj, local_sem.at[8]),
             pltpu.make_async_copy(mproj_hbm, mproj, local_sem.at[9]),
@@ -145,7 +148,7 @@
                     fw_hbm.at[a], fw.at[:, pl.ds(128 * a, 128), :], local_sem.at[3 + a]
                 )
             )
-        for copy in early + locals_:
+        for copy in locals_:
             copy.start()
         for copy in early:
             copy.wait()
@@ -293,7 +296,7 @@
                 edge_out[e, rr] = jnp.concatenate(both, axis=0).astype(BF16)
             return 0
 
-        lax.fori_loop(0, 8, edges, 0)
+        lax.fori_loop(0, 8, edges, 0, unroll=2)
         send(edge_out.at[0], edge_in.at[1], edge_sem.at[1], (g, left_t))
         send(edge_out.at[1], edge_in.at[0], edge_sem.at[0], (g, right_t))
         poll(POLLS[4])
@@ -308,7 +311,7 @@
                 )
             return 0
 
-        lax.fori_loop(0, 16, mains, 0)
+        lax.fori_loop(0, 16, mains, 0, unroll=2)
         poll(POLLS[5])
 
         def inside(condition, like):
@@ -423,7 +426,7 @@
             ).reshape(6, 4, 8, 256)
             return 0
 
-        lax.fori_loop(0, 9, mid_tap, 0)
+        lax.fori_loop(0, 9, mid_tap, 0, unroll=9)
 
         low = low.reshape(6, 4, 8, 256)
         for pr in range(2):

time: 59.2 us -> 57.8 us (0.976)
  Pallas kernels: 57.4 us -> 55.9 us
    pallas_call x1, Pallas kernels: 57.4 us -> 55.9 us  [body(): pl.pallas_call(make_kernel(nz), out_shape=jax.ShapeDtypeStruct((8, 16, 8,...]
where the time goes in v4:
time: 57.8 us; the launch traced here: 57.6 us
  Pallas kernels  55.9 us (97%)
  local copies, waits for them, and re-layouts  1.67 us (3%)
    pallas_call x1, Pallas kernels, body(): pl.pallas_call(make_kernel(nz), out_shape=jax.ShapeDtypeStruct((8, 16, 8,...  55.9 us
    unnamed x1, local copies, waits for them, and re-layouts  1.67 us

profile of v4, /device:TPU:1, one launch (start us, length us, event | category | flops | bytes accessed | tf_op | source)
XLA Modules:
  0.0 57.6 jit_solution(13600826795102155847)
XLA Ops:
  0.0 55.9 %shard_map.64 = bf16[8,16,8,128]{3,2,1,0:T(8,128)(2,1)} custom-call(bf16[8,4,2,512]{3,2,1,0:T(2,128)(2,1)} %latent_hbm.1, bf16[3,9,32,512]{3,2,1,0:T(8,128)(2,1)} %bitcast.7, bf16[27,8,256]{2,1,0:T(8,128)(2,1)} %bitcast.9, bf16[3,9,128,128]{3,2,1,0:T(8,128)(2,1)} %bitcast.8, bf16[512,256]{1,0:T(8,128)(2,1)} %cproj_hbm.1, bf16[256,128]{1,0:T(8,128)(2,1)} %mproj_hbm.1), custom_call_target="tpu_custom_call" | custom-call | tf_op jit(solution)/shard_map/pallas_call | solution.py:509
  55.9 1.7 %copy.8 = bf16[8,16,8,128]{3,2,1,0:T(8,128)(2,1)} copy(bf16[8,16,8,128]{3,2,1,0:T(8,128)(2,1)} %shard_map.64) | data formatting | bytes 524288

commit v5 on v4

--- a/solution.py
+++ b/solution.py
@@ -13,7 +13,7 @@
 NG = 16
 NT_DIMS = (((1,), (1,)), ((), ()))
 NN_DIMS = (((1,), (0,)), ((), ()))
-POLLS = (3, 3, 3, 2, 2, 2, 3, 2, 4)
+POLLS = (4, 3, 3, 3, 2, 2, 3, 1, 3)
 SHIFTS = ((-1, 0, 0), (0, 0, 1))
 
 
@@ -296,7 +296,7 @@
                 edge_out[e, rr] = jnp.concatenate(both, axis=0).astype(BF16)
             return 0
 
-        lax.fori_loop(0, 8, edges, 0, unroll=2)
+        lax.fori_loop(0, 8, edges, 0, unroll=4)
         send(edge_out.at[0], edge_in.at[1], edge_sem.at[1], (g, left_t))
         send(edge_out.at[1], edge_in.at[0], edge_sem.at[0], (g, right_t))
         poll(POLLS[4])
@@ -311,7 +311,7 @@
                 )
             return 0
 
-        lax.fori_loop(0, 16, mains, 0, unroll=2)
+        lax.fori_loop(0, 16, mains, 0, unroll=8)
         poll(POLLS[5])
 
         def inside(condition, like):

time: 57.8 us -> 56.8 us (0.983)
  Pallas kernels: 55.9 us -> 55 us
    pallas_call x1, Pallas kernels: 55.9 us -> 55 us  [body(): pl.pallas_call(make_kernel(nz), out_shape=jax.ShapeDtypeStruct((8, 16, 8,...]
where the time goes in v5:
time: 56.8 us; the launch traced here: 56.7 us
  Pallas kernels  55 us (97%)
  local copies, waits for them, and re-layouts  1.67 us (3%)
    pallas_call x1, Pallas kernels, body(): pl.pallas_call(make_kernel(nz), out_shape=jax.ShapeDtypeStruct((8, 16, 8,...  55 us
    unnamed x1, local copies, waits for them, and re-layouts  1.67 us

profile of v5, /device:TPU:1, one launch (start us, length us, event | category | flops | bytes accessed | tf_op | source)
XLA Modules:
  0.0 56.7 jit_solution(18017789512277659741)
XLA Ops:
  0.0 55.0 %shard_map.64 = bf16[8,16,8,128]{3,2,1,0:T(8,128)(2,1)} custom-call(bf16[8,4,2,512]{3,2,1,0:T(2,128)(2,1)} %latent_hbm.1, bf16[3,9,32,512]{3,2,1,0:T(8,128)(2,1)} %bitcast.7, bf16[27,8,256]{2,1,0:T(8,128)(2,1)} %bitcast.9, bf16[3,9,128,128]{3,2,1,0:T(8,128)(2,1)} %bitcast.8, bf16[512,256]{1,0:T(8,128)(2,1)} %cproj_hbm.1, bf16[256,128]{1,0:T(8,128)(2,1)} %mproj_hbm.1), custom_call_target="tpu_custom_call" | custom-call | tf_op jit(solution)/shard_map/pallas_call | solution.py:509
  55.0 1.7 %copy.8 = bf16[8,16,8,128]{3,2,1,0:T(8,128)(2,1)} copy(bf16[8,16,8,128]{3,2,1,0:T(8,128)(2,1)} %shard_map.64) | data formatting | bytes 524288
